TPU v7x, 128 devices: a whole 4x4x4 slice. The times are simulated.
128 devices in a mesh: dp: 2 (over core), row: 8 (over z, y_lo), col: 8 (over x, y_hi).
Axes of the slice: x: 4, y: 4 (y_hi: 2, y_lo: 2; y = y_hi * 2 + y_lo), z: 4, core: 2. Of those that a mesh axis runs over, the one named last changes fastest.
Arguments:
- images: bfloat16 [5120, 1024], P(('dp', 'col'), 'row'), may hold values from -6 to 6
- norm_gain1: float32 [2, 1024], P(None, 'row'), may hold values from 0.25 to 1.75
- norm_bias1: float32 [2, 1024], P(None, 'row'), may hold values from -4 to 4
- w_qkv: bfloat16 [2, 1024, 3, 1024], P(None, 'row', None, 'col'), may hold values from -0.1875 to 0.1875
- qv_bias: float32 [2, 2, 1024], P(None, None, 'col'), may hold values from -4 to 4
- w_out: bfloat16 [2, 1024, 1024], P(None, 'col', 'row'), may hold values from -1.5 to 1.5
- out_bias: float32 [2, 1024], P(None, 'row'), may hold values from -4 to 4
- norm_gain2: float32 [2, 1024], P(None, 'row'), may hold values from 0.25 to 1.75
- norm_bias2: float32 [2, 1024], P(None, 'row'), may hold values from -4 to 4
- w_up: bfloat16 [2, 1024, 4096], P(None, 'row', 'col'), may hold values from -0.1875 to 0.1875
- up_bias: float32 [2, 4096], P(None, 'col'), may hold values from -4 to 4
- w_down: bfloat16 [2, 4096, 1024], P(None, 'col', 'row'), may hold values from -0.09375 to 0.09375
- down_bias: float32 [2, 1024], P(None, 'row'), may hold values from -4 to 4
- cotangent: bfloat16 [5120, 1024], P(('dp', 'col'), 'row'), may hold values from -6 to 6
Outputs:
- encoded: bfloat16 [5120, 1024], P(('dp', 'col'), 'row')
- grad_input: float32 [5120, 1024], P(('dp', 'col'), 'row')
- grad_qkv: float32 [2, 1024, 3, 1024], P(None, 'row', None, 'col')
- grad_out_proj: float32 [2, 1024, 1024], P(None, 'col', 'row')
- grad_up: float32 [2, 1024, 4096], P(None, 'row', 'col')
- grad_down: float32 [2, 4096, 1024], P(None, 'col', 'row')
- grad_gain1: float32 [2, 1024], P(None, 'row')
- grad_bias1: float32 [2, 1024], P(None, 'row')
- grad_qv_bias: float32 [2, 2, 1024], P(None, None, 'col')
- grad_out_bias: float32 [2, 1024], P(None, 'row')
- grad_gain2: float32 [2, 1024], P(None, 'row')
- grad_bias2: float32 [2, 1024], P(None, 'row')
- grad_up_bias: float32 [2, 4096], P(None, 'col')
- grad_down_bias: float32 [2, 1024], P(None, 'row')
All inputs are finite; a program needn't handle non-finite values.
Results may differ from a plain program's by a relative error of at most 0.038.
Values may be sent and summed in bfloat16 or wider, within the bound.
A program may use at most 128 MiB of HBM per device.

v0:
```python
import jax
import jax.numpy as jnp
from jax import lax
from jax.sharding import PartitionSpec as P

D = 1024
SEQ = 320
LAYERS = 2
HEAD_DIM = 64


norm_eps = 1e-06
root_half = 0.7071067811865476
inv_root_tau = 0.3989422804014327


def as_sent(value):

    def short(part):
        return part.astype(jnp.bfloat16) if part.dtype == jnp.float32 else part

    return jax.tree.map(short, value)


def contract_last(left, right):
    return lax.dot_general(
        left, right, (((1,), (1,)), ((), ())), preferred_element_type=jnp.float32
    )


def contract_first(left, right):
    return lax.dot_general(
        left, right, (((0,), (0,)), ((), ())), preferred_element_type=jnp.float32
    )


def norm_forward(resid, norm_gain, norm_shift):
    row_total, row_square = lax.psum(
        (jnp.sum(resid, axis=1), jnp.sum(resid * resid, axis=1)), "row"
    )
    center = row_total / D
    scaled = lax.rsqrt(row_square / D - center * center + norm_eps)
    normal = (resid - center[:, None]) * scaled[:, None]
    return ((normal * norm_gain + norm_shift).astype(jnp.bfloat16), normal, scaled)


def norm_backward(grad_out, normal, scaled, norm_gain):
    upstream = grad_out * norm_gain
    mean_part, proj_part = lax.psum(
        (jnp.sum(upstream, axis=1), jnp.sum(upstream * normal, axis=1)), "row"
    )
    grad_resid = scaled[:, None] * (
        upstream - mean_part[:, None] / D - normal * proj_part[:, None] / D
    )
    return (grad_resid, jnp.sum(grad_out * normal, axis=0), jnp.sum(grad_out, axis=0))


def gather_features(block):
    return lax.all_gather(block, "col", axis=0, tiled=True)


def gather_tokens(block):
    return lax.all_gather(block, "row", axis=0, tiled=True)


def gather_grads(block):
    return lax.all_gather(block, "col", axis=0, tiled=True)


def gather_grad_tokens(block):
    return lax.all_gather(block, "row", axis=0, tiled=True)


def head_sums(gathered, weight, own_rows):

    def partial_value(first_row, row_count):
        return jnp.dot(gathered, weight, preferred_element_type=jnp.float32)

    return lax.psum_scatter(
        partial_value(jnp.int32(0), lax.axis_size("row") * own_rows).astype(jnp.bfloat16),
        "row",
        scatter_dimension=0,
        tiled=True,
    ).astype(jnp.float32)


def token_sums(gathered, weight, own_rows):

    def partial_value(first_row, row_count):
        return jnp.dot(gathered, weight, preferred_element_type=jnp.float32)

    return lax.psum_scatter(
        partial_value(jnp.int32(0), lax.axis_size("col") * own_rows).astype(jnp.bfloat16),
        "col",
        scatter_dimension=0,
        tiled=True,
    ).astype(jnp.float32)


def grad_head_sums(gathered, weight, own_rows):

    def partial_value(first_row, row_count):
        return contract_last(gathered, weight)

    return lax.psum_scatter(
        partial_value(jnp.int32(0), lax.axis_size("row") * own_rows).astype(jnp.bfloat16),
        "row",
        scatter_dimension=0,
        tiled=True,
    ).astype(jnp.float32)


def grad_token_sums(gathered, weight, own_rows):

    def partial_value(first_row, row_count):
        return contract_last(gathered, weight)

    return lax.psum_scatter(
        partial_value(jnp.int32(0), lax.axis_size("col") * own_rows).astype(jnp.bfloat16),
        "col",
        scatter_dimension=0,
        tiled=True,
    ).astype(jnp.float32)


def attend(query, keys, values, images_here, heads_here):
    head_shape = (images_here, SEQ, heads_here, HEAD_DIM)
    scores = jnp.einsum(
        "bqhd,bkhd->bhqk",
        query.reshape(head_shape),
        keys.reshape(head_shape),
        preferred_element_type=jnp.float32,
    ) * HEAD_DIM ** (-0.5)
    largest = jnp.max(scores, axis=-1, keepdims=True)
    raised = jnp.exp(scores - largest)
    totals = jnp.sum(raised, axis=-1, keepdims=True)
    shares = (raised / totals).astype(jnp.bfloat16)
    mixed = jnp.einsum(
        "bhqk,bkhd->bqhd", shares, values.reshape(head_shape), preferred_element_type=jnp.float32
    )
    logsum = largest[..., 0] + jnp.log(totals[..., 0])
    return (mixed.reshape(query.shape).astype(jnp.bfloat16), logsum)


def attend_back(query, keys, values, logsum, mixed_grad, images_here, heads_here):
    head_shape = (images_here, SEQ, heads_here, HEAD_DIM)
    query_heads = query.reshape(head_shape)
    keys_heads = keys.reshape(head_shape)
    grad_heads = mixed_grad.reshape(head_shape)
    scores = jnp.einsum(
        "bqhd,bkhd->bhqk", query_heads, keys_heads, preferred_element_type=jnp.float32
    ) * HEAD_DIM ** (-0.5)
    shares = jnp.exp(scores - logsum[..., None])
    shares_grad = jnp.einsum(
        "bqhd,bkhd->bhqk",
        grad_heads,
        values.reshape(head_shape),
        preferred_element_type=jnp.float32,
    )
    values_grad = jnp.einsum(
        "bhqk,bqhd->bkhd",
        shares.astype(jnp.bfloat16),
        grad_heads,
        preferred_element_type=jnp.float32,
    )
    inner = jnp.sum(shares * shares_grad, axis=-1, keepdims=True)
    scores_grad = (shares * (shares_grad - inner)).astype(jnp.bfloat16)
    query_grad = jnp.einsum(
        "bhqk,bkhd->bqhd", scores_grad, keys_heads, preferred_element_type=jnp.float32
    ) * HEAD_DIM ** (-0.5)
    keys_grad = jnp.einsum(
        "bhqk,bqhd->bkhd", scores_grad, query_heads, preferred_element_type=jnp.float32
    ) * HEAD_DIM ** (-0.5)
    flat = query.shape
    return (
        query_grad.reshape(flat).astype(jnp.bfloat16),
        keys_grad.reshape(flat).astype(jnp.bfloat16),
        values_grad.reshape(flat).astype(jnp.bfloat16),
    )


def gelu_slope(before):
    return 0.5 * (1.0 + lax.erf(before * root_half)) + before * inv_root_tau * jnp.exp(
        -0.5 * before * before
    )


def place_slot(piece, slot_index, slot_count):
    width_own = piece.shape[-1]
    blank = jnp.zeros(piece.shape[:-1] + (width_own * slot_count,), jnp.float32)
    return lax.dynamic_update_slice_in_dim(blank, piece, slot_index * width_own, piece.ndim - 1)


def take_slot(whole, slot_index, width_own):
    return lax.dynamic_slice_in_dim(whole, slot_index * width_own, width_own, whole.ndim - 1)


def on_device(
    images,
    norm_gain1,
    norm_bias1,
    w_qkv,
    qv_bias,
    w_out,
    out_bias,
    norm_gain2,
    norm_bias2,
    w_up,
    up_bias,
    w_down,
    down_bias,
    cotangent,
):
    col_rows = images.shape[0]
    group_rows = col_rows * lax.axis_size("col")
    row_rows = group_rows // lax.axis_size("row")
    width_row = images.shape[1]
    width_col = w_out.shape[1]
    heads_here = width_col // HEAD_DIM
    images_here = row_rows // SEQ
    resid = images.astype(jnp.float32)
    saved = []
    for layer in range(LAYERS):
        qkv_weight = w_qkv[layer].reshape(width_row, 3 * width_col)
        normed, normal_one, scaled_one = norm_forward(resid, norm_gain1[layer], norm_bias1[layer])
        normed_all = gather_features(normed)
        projected = head_sums(normed_all, qkv_weight, row_rows)
        query = (projected[:, :width_col] + qv_bias[layer, 0]).astype(jnp.bfloat16)
        keys = projected[:, width_col : 2 * width_col].astype(jnp.bfloat16)
        values = (projected[:, 2 * width_col :] + qv_bias[layer, 1]).astype(jnp.bfloat16)
        mixed, logsum = attend(query, keys, values, images_here, heads_here)
        mixed_all = gather_tokens(mixed)
        attn_out = token_sums(mixed_all, w_out[layer], col_rows)
        middle = resid + attn_out + out_bias[layer]
        normed_two, normal_two, scaled_two = norm_forward(
            middle, norm_gain2[layer], norm_bias2[layer]
        )
        normed_two_all = gather_features(normed_two)
        before = head_sums(normed_two_all, w_up[layer], row_rows) + up_bias[layer]
        hidden = jax.nn.gelu(before, approximate=False).astype(jnp.bfloat16)
        hidden_all = gather_tokens(hidden)
        mlp_out = token_sums(hidden_all, w_down[layer], col_rows)
        resid = middle + mlp_out + down_bias[layer]
        kept_mixed = mixed_all
        kept_hidden = hidden_all
        saved.append(
            (
                normed_all,
                normal_one,
                scaled_one,
                query,
                keys,
                values,
                logsum,
                kept_mixed,
                normed_two_all,
                normal_two,
                scaled_two,
                before,
                kept_hidden,
            )
        )
    grad = cotangent.astype(jnp.float32)
    weight_terms = [None] * LAYERS
    vector_terms = [None] * LAYERS
    for layer in reversed(range(LAYERS)):
        (
            normed_all,
            normal_one,
            scaled_one,
            query,
            keys,
            values,
            logsum,
            kept_mixed,
            normed_two_all,
            normal_two,
            scaled_two,
            before,
            kept_hidden,
        ) = saved[layer]
        qkv_weight = w_qkv[layer].reshape(width_row, 3 * width_col)
        mixed_all = kept_mixed
        hidden_all = kept_hidden
        branch_two = grad.astype(jnp.bfloat16)
        down_shift_grad = jnp.sum(branch_two.astype(jnp.float32), axis=0)
        branch_two_all = gather_grads(branch_two)
        down_grad = contract_first(hidden_all, branch_two_all)
        hidden_grad = grad_head_sums(branch_two_all, w_down[layer], row_rows)
        before_grad = (hidden_grad * gelu_slope(before)).astype(jnp.bfloat16)
        up_shift_grad = jnp.sum(before_grad.astype(jnp.float32), axis=0)
        before_all = gather_grad_tokens(before_grad)
        up_grad = contract_first(normed_two_all, before_all)
        normed_two_grad = grad_token_sums(before_all, w_up[layer], col_rows)
        resid_grad, gain_two_grad, shift_two_grad = norm_backward(
            normed_two_grad, normal_two, scaled_two, norm_gain2[layer]
        )
        grad_mid = grad + resid_grad
        branch_one = grad_mid.astype(jnp.bfloat16)
        out_shift_grad = jnp.sum(branch_one.astype(jnp.float32), axis=0)
        branch_one_all = gather_grads(branch_one)
        out_grad = contract_first(mixed_all, branch_one_all)
        mixed_grad = grad_head_sums(branch_one_all, w_out[layer], row_rows).astype(jnp.bfloat16)
        query_grad, keys_grad, values_grad = attend_back(
            query, keys, values, logsum, mixed_grad, images_here, heads_here
        )
        qv_shift_grad = jnp.stack(
            [
                jnp.sum(query_grad.astype(jnp.float32), axis=0),
                jnp.sum(values_grad.astype(jnp.float32), axis=0),
            ]
        )
        joined = jnp.concatenate([query_grad, keys_grad, values_grad], axis=1)
        joined_all = gather_grad_tokens(joined)
        qkv_grad = contract_first(normed_all, joined_all)
        normed_one_grad = grad_token_sums(joined_all, qkv_weight, col_rows)
        resid_grad, gain_one_grad, shift_one_grad = norm_backward(
            normed_one_grad, normal_one, scaled_one, norm_gain1[layer]
        )
        grad = grad_mid + resid_grad
        layer_grads = (qkv_grad, out_grad, up_grad, down_grad)
        weight_terms[layer] = layer_grads
        vector_terms[layer] = (
            gain_one_grad,
            shift_one_grad,
            qv_shift_grad,
            out_shift_grad,
            gain_two_grad,
            shift_two_grad,
            up_shift_grad,
            down_shift_grad,
        )
    stacked = tuple(
        (jnp.stack([weight_terms[layer][member] for layer in range(LAYERS)]) for member in range(4))
    )
    stacked = jax.tree.map(lambda part: part.astype(jnp.float32), lax.psum(as_sent(stacked), "dp"))
    row_slot = lax.axis_index("row")
    col_slot = lax.axis_index("col")
    row_count = lax.axis_size("row")
    col_count = lax.axis_size("col")
    on_cols = (2, 6)
    partials = []
    for member in range(8):
        piece = jnp.stack([vector_terms[layer][member] for layer in range(LAYERS)])
        if member in on_cols:
            partials.append(place_slot(piece, col_slot, col_count))
        else:
            partials.append(place_slot(piece, row_slot, row_count))
    summed = lax.psum(tuple(partials), ("dp", "row", "col"))
    vectors = []
    for member in range(8):
        if member in on_cols:
            vectors.append(
                take_slot(summed[member], col_slot, summed[member].shape[-1] // col_count)
            )
        else:
            vectors.append(
                take_slot(summed[member], row_slot, summed[member].shape[-1] // row_count)
            )
    return (
        resid.astype(jnp.bfloat16),
        grad,
        stacked[0].reshape(LAYERS, width_row, 3, width_col),
        stacked[1],
        stacked[2],
        stacked[3],
        vectors[0],
        vectors[1],
        vectors[2],
        vectors[3],
        vectors[4],
        vectors[5],
        vectors[6],
        vectors[7],
    )


def solution(mesh):
    return jax.shard_map(
        on_device,
        mesh=mesh,
        in_specs=(
            P(("dp", "col"), "row"),
            P(None, "row"),
            P(None, "row"),
            P(None, "row", None, "col"),
            P(None, None, "col"),
            P(None, "col", "row"),
            P(None, "row"),
            P(None, "row"),
            P(None, "row"),
            P(None, "row", "col"),
            P(None, "col"),
            P(None, "col", "row"),
            P(None, "row"),
            P(("dp", "col"), "row"),
        ),
        out_specs=(
            P(("dp", "col"), "row"),
            P(("dp", "col"), "row"),
            P(None, "row", None, "col"),
            P(None, "col", "row"),
            P(None, "row", "col"),
            P(None, "col", "row"),
            P(None, "row"),
            P(None, "row"),
            P(None, None, "col"),
            P(None, "row"),
            P(None, "row"),
            P(None, "row"),
            P(None, "col"),
            P(None, "row"),
        ),
        check_vma=False,
    )
```

profile of v0, /device:TPU:1, one launch (start us, length us, event | category | flops | bytes accessed | tf_op | source)
XLA Modules:
  0.0 2011.1 jit_solution(11331185292005041924)
XLA Ops:
  10.2 18.2 all-reduce.8
  29.4 29.8 %all_gather.48 = bf16[2560,128]{1,0:T(8,128)(2,1)S(1)} all-gather(bf16[320,128]{1,0:T(8,128)(2,1)S(1)} %fusion.91), channel_id=1, replica_groups=mesh['dp'=2,'row'=8,'col'=8] {'col'}, dimensions={0}, use_global_device_ids=true | all-gather | bytes 737280 | tf_op jit(solution)/shard_map/all_gather | solution.py:59
  59.3 2.0 convolution_convert_fusion.5
  61.4 57.9 %reduce-scatter.17.cloned.1.call-done = bf16[320,384]{1,0:T(8,128)(2,1)} async-done(((bf16[2560,384]{1,0:T(8,128)(2,1)}), bf16[320,384]{1,0:T(8,128)(2,1)}) %reduce-scatter.17.cloned.1.call-update) | async-done | bytes 245776 | tf_op jit(solution)/shard_map/reduce_scatter | solution.py:79
  122.6 25.5 %all_gather.49 = bf16[2560,128]{1,0:T(8,128)(2,1)S(1)} all-gather(bf16[320,128]{1,0:T(8,128)(2,1)S(1)} %copy.78), channel_id=1, replica_groups=mesh['dp'=2,'row'=8,'col'=8] {'row'}, dimensions={0}, use_global_device_ids=true | all-gather | bytes 737280 | tf_op jit(solution)/shard_map/all_gather | solution.py:63
  150.4 72.2 %reduce-scatter.19.cloned.1.call-done = bf16[320,128]{1,0:T(8,128)(2,1)} async-done(((bf16[2560,128]{1,0:T(8,128)(2,1)}), bf16[320,128]{1,0:T(8,128)(2,1)}) %reduce-scatter.19.cloned.1.call-update) | async-done | bytes 81936 | tf_op jit(solution)/shard_map/reduce_scatter | solution.py:92
  223.7 15.7 all-reduce.7
  240.5 29.7 %all_gather.50 = bf16[2560,128]{1,0:T(8,128)(2,1)S(1)} all-gather(bf16[320,128]{1,0:T(8,128)(2,1)S(1)} %add_convert_fusion.3), channel_id=1, replica_groups=mesh['dp'=2,'row'=8,'col'=8] {'col'}, dimensions={0}, use_global_device_ids=true | all-gather | bytes 737280 | tf_op jit(solution)/shard_map/all_gather | solution.py:59
  271.0 2.3 convolution_convert_fusion.3
  274.0 69.9 %reduce-scatter.21.cloned.1.call-done = bf16[320,512]{1,0:T(8,128)(2,1)} async-done(((bf16[2560,512]{1,0:T(8,128)(2,1)}), bf16[320,512]{1,0:T(8,128)(2,1)}) %reduce-scatter.21.cloned.1.call-update) | async-done | bytes 327696 | tf_op jit(solution)/shard_map/reduce_scatter | solution.py:79
  343.9 3.2 fusion.18
  347.2 61.3 %all-gather.7.cloned.1.call-done = bf16[2560,512]{1,0:T(8,128)(2,1)} async-done(((bf16[320,512]{1,0:T(8,128)(2,1)}), bf16[2560,512]{1,0:T(8,128)(2,1)}) %all-gather.7.cloned.1.call-update) | async-done | bytes 2621456 | tf_op jit(solution)/shard_map/all_gather | solution.py:63
  408.5 3.4 convolution_convert_fusion.12
  412.7 68.8 %reduce-scatter.23.cloned.1.call-done = bf16[320,128]{1,0:T(8,128)(2,1)} async-done(((bf16[2560,128]{1,0:T(8,128)(2,1)}), bf16[320,128]{1,0:T(8,128)(2,1)}) %reduce-scatter.23.cloned.1.call-update) | async-done | bytes 81936 | tf_op jit(solution)/shard_map/reduce_scatter | solution.py:92
  482.6 15.7 all-reduce.6
  498.5 29.2 %all_gather.52 = bf16[2560,128]{1,0:T(8,128)(2,1)S(1)} all-gather(bf16[320,128]{1,0:T(8,128)(2,1)S(1)} %add_convert_fusion.2), channel_id=1, replica_groups=mesh['dp'=2,'row'=8,'col'=8] {'col'}, dimensions={0}, use_global_device_ids=true | all-gather | bytes 737280 | tf_op jit(solution)/shard_map/all_gather | solution.py:59
  528.5 2.0 convolution_convert_fusion.4
  530.6 58.7 %reduce-scatter.25.cloned.1.call-done = bf16[320,384]{1,0:T(8,128)(2,1)} async-done(((bf16[2560,384]{1,0:T(8,128)(2,1)}), bf16[320,384]{1,0:T(8,128)(2,1)}) %reduce-scatter.25.cloned.1.call-update) | async-done | bytes 245776 | tf_op jit(solution)/shard_map/reduce_scatter | solution.py:79
  594.3 1.9 convolution_convert_fusion.24
  597.2 24.8 %all_gather.53 = bf16[2560,128]{1,0:T(8,128)(2,1)S(1)} all-gather(bf16[320,128]{1,0:T(8,128)(2,1)S(1)} %copy.84), channel_id=1, replica_groups=mesh['dp'=2,'row'=8,'col'=8] {'row'}, dimensions={0}, use_global_device_ids=true | all-gather | bytes 737280 | tf_op jit(solution)/shard_map/all_gather | solution.py:63
  624.1 30.6 %all_gather.56 = bf16[2560,128]{1,0:T(8,128)(2,1)S(1)} all-gather(bf16[320,128]{1,0:T(8,128)(2,1)S(1)} %copy-done.37), channel_id=1, replica_groups=mesh['dp'=2,'row'=8,'col'=8] {'col'}, dimensions={0}, use_global_device_ids=true | all-gather | bytes 737280 | tf_op jit(solution)/shard_map/all_gather | solution.py:67
  655.5 2.4 convolution_convert_fusion.1
  658.0 40.6 %reduce-scatter.27.cloned.1.call-done = bf16[320,128]{1,0:T(8,128)(2,1)} async-done(((bf16[2560,128]{1,0:T(8,128)(2,1)}), bf16[320,128]{1,0:T(8,128)(2,1)}) %reduce-scatter.27.cloned.1.call-update) | async-done | bytes 81936 | tf_op jit(solution)/shard_map/reduce_scatter | solution.py:92
  700.2 16.8 all-reduce.5
  719.2 31.7 %all_gather.54 = bf16[2560,128]{1,0:T(8,128)(2,1)S(1)} all-gather(bf16[320,128]{1,0:T(8,128)(2,1)S(1)} %add_convert_fusion.1), channel_id=1, replica_groups=mesh['dp'=2,'row'=8,'col'=8] {'col'}, dimensions={0}, use_global_device_ids=true | all-gather | bytes 737280 | tf_op jit(solution)/shard_map/all_gather | solution.py:59
  751.7 3.2 convolution_convert_fusion.2
  755.0 21.6 %reduce-scatter.33.cloned.1.call-done = bf16[320,512]{1,0:T(8,128)(2,1)} async-done(((bf16[2560,512]{1,0:T(8,128)(2,1)}), bf16[320,512]{1,0:T(8,128)(2,1)}) %reduce-scatter.33.cloned.1.call-update) | async-done | bytes 327696 | tf_op jit(solution)/shard_map/reduce_scatter | solution.py:105
  776.7 64.1 %reduce-scatter.29.cloned.1.call-done = bf16[320,512]{1,0:T(8,128)(2,1)} async-done(((bf16[2560,512]{1,0:T(8,128)(2,1)}), bf16[320,512]{1,0:T(8,128)(2,1)}) %reduce-scatter.29.cloned.1.call-update) | async-done | bytes 327696 | tf_op jit(solution)/shard_map/reduce_scatter | solution.py:79
  840.7 4.2 convert_reduce_fusion
  845.8 60.6 %all-gather.11.cloned.1.call-done = bf16[2560,512]{1,0:T(8,128)(2,1)} async-done(((bf16[320,512]{1,0:T(8,128)(2,1)}), bf16[2560,512]{1,0:T(8,128)(2,1)}) %all-gather.11.cloned.1.call-update) | async-done | bytes 2621456 | tf_op jit(solution)/shard_map/all_gather | solution.py:71
  906.4 3.5 convolution_convert_fusion.9
  910.0 60.0 %all-gather.9.cloned.1.call-done = bf16[2560,512]{1,0:T(8,128)(2,1)} async-done(((bf16[320,512]{1,0:T(8,128)(2,1)}), bf16[2560,512]{1,0:T(8,128)(2,1)}) %all-gather.9.cloned.1.call-update) | async-done | bytes 2621456 | tf_op jit(solution)/shard_map/all_gather | solution.py:63
  969.9 3.5 convolution_convert_fusion.10
  973.5 69.0 %reduce-scatter.35.cloned.1.call-done = bf16[320,128]{1,0:T(8,128)(2,1)} async-done(((bf16[2560,128]{1,0:T(8,128)(2,1)}), bf16[320,128]{1,0:T(8,128)(2,1)}) %reduce-scatter.35.cloned.1.call-update) | async-done | bytes 81936 | tf_op jit(solution)/shard_map/reduce_scatter | solution.py:118
  1044.3 16.1 all-reduce.4
  1061.7 55.1 %reduce-scatter.31.cloned.1.call-done = bf16[320,128]{1,0:T(8,128)(2,1)} async-done(((bf16[2560,128]{1,0:T(8,128)(2,1)}), bf16[320,128]{1,0:T(8,128)(2,1)}) %reduce-scatter.31.cloned.1.call-update) | async-done | bytes 81936 | tf_op jit(solution)/shard_map/reduce_scatter | solution.py:92
  1116.7 2.4 convert_reduce_fusion.13
  1119.2 29.4 %all_gather.58 = bf16[2560,128]{1,0:T(8,128)(2,1)S(1)} all-gather(bf16[320,128]{1,0:T(8,128)(2,1)S(1)} %get-tuple-element.105), channel_id=1, replica_groups=mesh['dp'=2,'row'=8,'col'=8] {'col'}, dimensions={0}, use_global_device_ids=true | all-gather | bytes 737280 | tf_op jit(solution)/shard_map/all_gather | solution.py:67
  1149.5 2.0 convolution_convert_fusion.8
  1151.6 40.7 %reduce-scatter.37.cloned.1.call-done = bf16[320,128]{1,0:T(8,128)(2,1)} async-done(((bf16[2560,128]{1,0:T(8,128)(2,1)}), bf16[320,128]{1,0:T(8,128)(2,1)}) %reduce-scatter.37.cloned.1.call-update) | async-done | bytes 81936 | tf_op jit(solution)/shard_map/reduce_scatter | solution.py:105
  1198.4 53.5 %all-gather.13.cloned.1.call-done = bf16[2560,384]{1,0:T(8,128)(2,1)} async-done(((bf16[320,384]{1,0:T(8,128)(2,1)}), bf16[2560,384]{1,0:T(8,128)(2,1)}) %all-gather.13.cloned.1.call-update) | async-done | bytes 1966096 | tf_op jit(solution)/shard_map/all_gather | solution.py:71
  1251.9 3.1 convolution_convert_fusion.15
  1255.0 69.2 %reduce-scatter.39.cloned.1.call-done = bf16[320,128]{1,0:T(8,128)(2,1)} async-done(((bf16[2560,128]{1,0:T(8,128)(2,1)}), bf16[320,128]{1,0:T(8,128)(2,1)}) %reduce-scatter.39.cloned.1.call-update) | async-done | bytes 81936 | tf_op jit(solution)/shard_map/reduce_scatter | solution.py:118
  1325.5 15.7 all-reduce.3
  1342.3 29.8 %all_gather.60 = bf16[2560,128]{1,0:T(8,128)(2,1)S(1)} all-gather(bf16[320,128]{1,0:T(8,128)(2,1)S(1)} %get-tuple-element.95), channel_id=1, replica_groups=mesh['dp'=2,'row'=8,'col'=8] {'col'}, dimensions={0}, use_global_device_ids=true | all-gather | bytes 737280 | tf_op jit(solution)/shard_map/all_gather | solution.py:67
  1372.9 2.4 convolution_convert_fusion
  1375.4 70.5 %reduce-scatter.41.cloned.1.call-done = bf16[320,512]{1,0:T(8,128)(2,1)} async-done(((bf16[2560,512]{1,0:T(8,128)(2,1)}), bf16[320,512]{1,0:T(8,128)(2,1)}) %reduce-scatter.41.cloned.1.call-update) | async-done | bytes 327696 | tf_op jit(solution)/shard_map/reduce_scatter | solution.py:105
  1445.9 2.1 convert_reduce_fusion.1
  1448.1 61.3 %all-gather.15.cloned.1.call-done = bf16[2560,512]{1,0:T(8,128)(2,1)} async-done(((bf16[320,512]{1,0:T(8,128)(2,1)}), bf16[2560,512]{1,0:T(8,128)(2,1)}) %all-gather.15.cloned.1.call-update) | async-done | bytes 2621456 | tf_op jit(solution)/shard_map/all_gather | solution.py:71
  1509.4 3.5 convolution_convert_fusion.7
  1512.9 69.2 %reduce-scatter.43.cloned.1.call-done = bf16[320,128]{1,0:T(8,128)(2,1)} async-done(((bf16[2560,128]{1,0:T(8,128)(2,1)}), bf16[320,128]{1,0:T(8,128)(2,1)}) %reduce-scatter.43.cloned.1.call-update) | async-done | bytes 81936 | tf_op jit(solution)/shard_map/reduce_scatter | solution.py:118
  1583.3 15.4 all-reduce.2
  1599.9 29.8 %all_gather.62 = bf16[2560,128]{1,0:T(8,128)(2,1)S(1)} all-gather(bf16[320,128]{1,0:T(8,128)(2,1)S(1)} %get-tuple-element.102), channel_id=1, replica_groups=mesh['dp'=2,'row'=8,'col'=8] {'col'}, dimensions={0}, use_global_device_ids=true | all-gather | bytes 737280 | tf_op jit(solution)/shard_map/all_gather | solution.py:67
  1632.0 42.0 %reduce-scatter.45.cloned.1.call-done = bf16[320,128]{1,0:T(8,128)(2,1)} async-done(((bf16[2560,128]{1,0:T(8,128)(2,1)}), bf16[320,128]{1,0:T(8,128)(2,1)}) %reduce-scatter.45.cloned.1.call-update) | async-done | bytes 81936 | tf_op jit(solution)/shard_map/reduce_scatter | solution.py:105
  1677.8 2.6 fusion.5
  1680.4 2.9 fusion.7
  1689.5 41.7 %all-gather.17.cloned.1.call-done = bf16[2560,384]{1,0:T(8,128)(2,1)} async-done(((bf16[320,384]{1,0:T(8,128)(2,1)}), bf16[2560,384]{1,0:T(8,128)(2,1)}) %all-gather.17.cloned.1.call-update) | async-done | bytes 1966096 | tf_op jit(solution)/shard_map/all_gather | solution.py:71
  1731.2 2.4 fusion.8
  1736.9 22.3 %all-reduce.15.cloned.1.call-done = (bf16[2,128,3,128]{1,3,2,0:T(8,128)(2,1)}, bf16[2,128,128]{2,1,0:T(8,128)(2,1)}, bf16[2,128,512]{2,1,0:T(8,128)(2,1)}, bf16[2,512,128]{2,1,0:T(8,128)(2,1)}) async-done(((bf16[2,128,3,128]{1,3,2,0:T(8,128)(2,1)}, bf16[2,128,128]{2,1,0:T(8,128)(2,1)}, bf16[2,128,512]{2,1,0:T(8,128)(2,1)}, bf16[2,512,128]{2,1,0:T(8,128)(2,1)}), (bf16[2,128,3,128]{1,3,2,0:T(8,128)(2,1)}, ...) | async-done | bytes 786448 | tf_op jit(solution)/shard_map/psum | solution.py:336
  1760.7 1.8 copy.100
  1762.5 1.8 convert_element_type.424
  1766.1 67.7 %reduce-scatter.47.cloned.1.call-done = bf16[320,128]{1,0:T(8,128)(2,1)} async-done(((bf16[2560,128]{1,0:T(8,128)(2,1)}), bf16[320,128]{1,0:T(8,128)(2,1)}) %reduce-scatter.47.cloned.1.call-update) | async-done | bytes 81936 | tf_op jit(solution)/shard_map/reduce_scatter | solution.py:118
  1835.0 15.4 all-reduce.1
  1853.0 141.4 %all-reduce.13.cloned.1.call-done = (f32[2,1024]{1,0:T(2,128)}, f32[2,1024]{1,0:T(2,128)}, f32[2,2,1024]{2,1,0:T(2,128)}, f32[2,1024]{1,0:T(2,128)}, f32[2,1024]...) async-done(((f32[2,1024]{1,0:T(2,128)}, f32[2,1024]{1,0:T(2,128)}, f32[2,2,1024]{2,1,0:T(2,128)}, f32[2,1024]{1,0:T(2,128)}, ...) | async-done | bytes 98320 | tf_op jit(solution)/shard_map/psum | solution.py:349
  (349 shorter events, 78.5 us)
Async XLA Ops:
  7.2 112.1 %reduce-scatter.17.cloned.1.call-start = ((), (), s32[]{:S(2)}) async-start(), calls=%async_computation.16 | async-start | bytes 2211840 | tf_op jit(solution)/shard_map/reduce_scatter | solution.py:79
  9.4 51.9 %copy-start.30 = (bf16[1,128,3,128]{1,3,2,0:T(8,128)(2,1)}, bf16[1,128,3,128]{1,3,2,0:T(8,128)(2,1)S(1)}, u32[]{:S(2)}) copy-start(bf16[1,128,3,128]{1,3,2,0:T(8,128)(2,1)S(1)} %copy.109) | copy-start | bytes 294916
  10.2 51.1 %copy-start.74 = (f32[128]{0:T(128)}, f32[128]{0:T(128)S(1)}, u32[]{:S(2)}) copy-start(f32[128]{0:T(128)S(1)} %get-tuple-element.160) | copy-start | bytes 1540
  10.2 488.1 %copy-start.79 = (f32[128]{0:T(128)}, f32[128]{0:T(128)S(1)}, u32[]{:S(2)}) copy-start(f32[128]{0:T(128)S(1)} %get-tuple-element.161) | copy-start | bytes 1540
  28.3 33.0 %copy-start.44 = (f32[320]{0:T(512)}, f32[320]{0:T(512)S(1)}, u32[]{:S(2)}) copy-start(f32[320]{0:T(512)S(1)} %get-tuple-element.131) | copy-start | bytes 3844
  59.3 62.0 %copy-start.11 = (bf16[2560,128]{1,0:T(8,128)(2,1)}, bf16[2560,128]{1,0:T(8,128)(2,1)S(1)}, u32[]{:S(2)}) copy-start(bf16[2560,128]{1,0:T(8,128)(2,1)S(1)} %all_gather.48) | copy-start | bytes 1966084
  61.3 161.3 %reduce-scatter.19.cloned.1.call-start = ((), (), s32[]{:S(2)}) async-start(), calls=%async_computation.17 | async-start | bytes 737280 | tf_op jit(solution)/shard_map/reduce_scatter | solution.py:92
  122.2 100.5 %copy-start.4 = (bf16[320,128]{1,0:T(8,128)(2,1)S(1)}, bf16[320,128]{1,0:T(8,128)(2,1)}, u32[]{:S(2)}) copy-start(bf16[320,128]{1,0:T(8,128)(2,1)} %param.14) | copy-start | bytes 245764
  122.5 148.5 %copy-start.23 = (bf16[2,128,512]{2,1,0:T(8,128)(2,1)S(1)}, bf16[2,128,512]{2,1,0:T(8,128)(2,1)}, u32[]{:S(2)}) copy-start(bf16[2,128,512]{2,1,0:T(8,128)(2,1)} %param.23) | copy-start | bytes 786436
  149.3 194.6 %reduce-scatter.21.cloned.1.call-start = ((), (), s32[]{:S(2)}) async-start(), calls=%async_computation.18 | async-start | bytes 2949120 | tf_op jit(solution)/shard_map/reduce_scatter | solution.py:79
  149.9 331.6 %copy-start.66 = (f32[128]{0:T(128)}, f32[128]{0:T(128)S(1)}, u32[]{:S(2)}) copy-start(f32[128]{0:T(128)S(1)} %get-tuple-element.142) | copy-start | bytes 1540
  150.4 123.0 %copy-start.76 = (f32[128]{0:T(128)}, f32[128]{0:T(128)S(1)}, u32[]{:S(2)}) copy-start(f32[128]{0:T(128)S(1)} %get-tuple-element.162) | copy-start | bytes 1540
  273.4 135.2 %copy-start.22 = (bf16[2,512,128]{2,1,0:T(8,128)(2,1)S(1)}, bf16[2,512,128]{2,1,0:T(8,128)(2,1)}, u32[]{:S(2)}) copy-start(bf16[2,512,128]{2,1,0:T(8,128)(2,1)} %param.25) | copy-start | bytes 786436
  273.4 135.1 %all-gather.7.cloned.1.call-start = ((), (), s32[]{:S(2)}) async-start(), calls=%async_computation.19 | async-start | bytes 2949120 | tf_op jit(solution)/shard_map/all_gather | solution.py:63
  274.0 73.0 %copy-start.68 = (f32[1,512]{1,0:T(1,128)}, f32[1,512]{1,0:T(1,128)S(1)}, u32[]{:S(2)}) copy-start(f32[1,512]{1,0:T(1,128)S(1)} %get-tuple-element.119) | copy-start | bytes 6148
  347.1 65.0 %copy-start.88 = (f32[2,128]{1,0:T(2,128)S(1)}, f32[2,128]{1,0:T(2,128)}, u32[]{:S(2)}) copy-start(f32[2,128]{1,0:T(2,128)} %param.26) | copy-start | bytes 3076
  347.1 134.4 %copy-start.20 = (bf16[320,128]{1,0:T(8,128)(2,1)S(1)}, bf16[320,128]{1,0:T(8,128)(2,1)}, u32[]{:S(2)}) copy-start(bf16[320,128]{1,0:T(8,128)(2,1)} %reduce-scatter.19.cloned.1.call-done) | copy-start | bytes 245764
  347.1 134.4 %reduce-scatter.23.cloned.1.call-start = ((), (), s32[]{:S(2)}) async-start(), calls=%async_computation.20 | async-start | bytes 737280 | tf_op jit(solution)/shard_map/reduce_scatter | solution.py:92
  412.0 177.3 %reduce-scatter.25.cloned.1.call-start = ((), (), s32[]{:S(2)}) async-start(), calls=%async_computation.21 | async-start | bytes 2211840 | tf_op jit(solution)/shard_map/reduce_scatter | solution.py:79
  412.2 118.4 %copy-start.32 = (bf16[1,128,3,128]{1,3,2,0:T(8,128)(2,1)}, bf16[1,128,3,128]{1,3,2,0:T(8,128)(2,1)S(1)}, u32[]{:S(2)}) copy-start(bf16[1,128,3,128]{1,3,2,0:T(8,128)(2,1)S(1)} %copy.110) | copy-start | bytes 294916
  530.5 168.0 %reduce-scatter.27.cloned.1.call-start = ((), (), s32[]{:S(2)}) async-start(), calls=%async_computation.22 | async-start | bytes 737280 | tf_op jit(solution)/shard_map/reduce_scatter | solution.py:92
  624.0 152.6 %reduce-scatter.33.cloned.1.call-start = ((), (), s32[]{:S(2)}) async-start(), calls=%async_computation.26 | async-start | bytes 2949120 | tf_op jit(solution)/shard_map/reduce_scatter | solution.py:105
  657.9 182.8 %reduce-scatter.29.cloned.1.call-start = ((), (), s32[]{:S(2)}) async-start(), calls=%async_computation.23 | async-start | bytes 2949120 | tf_op jit(solution)/shard_map/reduce_scatter | solution.py:79
  755.0 151.4 %all-gather.11.cloned.1.call-start = ((), (), s32[]{:S(2)}) async-start(), calls=%async_computation.27 | async-start | bytes 2949120 | tf_op jit(solution)/shard_map/all_gather | solution.py:71
  845.0 124.9 %all-gather.9.cloned.1.call-start = ((), (), s32[]{:S(2)}) async-start(), calls=%async_computation.24 | async-start | bytes 2949120 | tf_op jit(solution)/shard_map/all_gather | solution.py:63
  845.7 196.8 %reduce-scatter.35.cloned.1.call-start = ((), (), s32[]{:S(2)}) async-start(), calls=%async_computation.28 | async-start | bytes 737280 | tf_op jit(solution)/shard_map/reduce_scatter | solution.py:118
  909.9 206.8 %reduce-scatter.31.cloned.1.call-start = ((), (), s32[]{:S(2)}) async-start(), calls=%async_computation.25 | async-start | bytes 737280 | tf_op jit(solution)/shard_map/reduce_scatter | solution.py:92
  973.4 218.8 %reduce-scatter.37.cloned.1.call-start = ((), (), s32[]{:S(2)}) async-start(), calls=%async_computation.29 | async-start | bytes 737280 | tf_op jit(solution)/shard_map/reduce_scatter | solution.py:105
  1151.5 100.4 %all-gather.13.cloned.1.call-start = ((), (), s32[]{:S(2)}) async-start(), calls=%async_computation.30 | async-start | bytes 2211840 | tf_op jit(solution)/shard_map/all_gather | solution.py:71
  1195.5 56.4 %copy-start.33 = (bf16[1,128,3,128]{1,3,2,0:T(8,128)(2,1)S(1)}, bf16[1,128,3,128]{1,3,2,0:T(8,128)(2,1)}, u32[]{:S(2)}) copy-start(bf16[1,128,3,128]{1,3,2,0:T(8,128)(2,1)} %copy-done.32) | copy-start | bytes 294916
  1196.0 128.3 %copy-start.51 = (f32[320]{0:T(512)S(1)}, f32[320]{0:T(512)}, u32[]{:S(2)}) copy-start(f32[320]{0:T(512)} %copy-done.50) | copy-start | bytes 3844
  1196.0 128.3 %copy-start.53 = (f32[320]{0:T(512)S(1)}, f32[320]{0:T(512)}, u32[]{:S(2)}) copy-start(f32[320]{0:T(512)} %copy-done.52) | copy-start | bytes 3844
  1196.0 128.3 %copy-start.80 = (f32[128]{0:T(128)S(1)}, f32[128]{0:T(128)}, u32[]{:S(2)}) copy-start(f32[128]{0:T(128)} %copy-done.79) | copy-start | bytes 1540
  1196.3 144.8 %copy-start.34 = (f32[320,128]{1,0:T(8,128)S(1)}, f32[320,128]{1,0:T(8,128)}, u32[]{:S(2)}) copy-start(f32[320,128]{1,0:T(8,128)} %get-tuple-element.106) | copy-start | bytes 491524
  1198.4 125.9 %reduce-scatter.39.cloned.1.call-start = ((), (), s32[]{:S(2)}) async-start(), calls=%async_computation.31 | async-start | bytes 737280 | tf_op jit(solution)/shard_map/reduce_scatter | solution.py:118
  1255.0 190.9 %reduce-scatter.41.cloned.1.call-start = ((), (), s32[]{:S(2)}) async-start(), calls=%async_computation.32 | async-start | bytes 2949120 | tf_op jit(solution)/shard_map/reduce_scatter | solution.py:105
  1372.9 73.0 %copy-start.21 = (bf16[320,512]{1,0:T(8,128)(2,1)S(1)}, bf16[320,512]{1,0:T(8,128)(2,1)}, u32[]{:S(2)}) copy-start(bf16[320,512]{1,0:T(8,128)(2,1)} %reduce-scatter.21.cloned.1.call-done) | copy-start | bytes 983044
  1372.9 73.0 %copy-start.69 = (f32[1,512]{1,0:T(1,128)S(1)}, f32[1,512]{1,0:T(1,128)}, u32[]{:S(2)}) copy-start(f32[1,512]{1,0:T(1,128)} %copy-done.68) | copy-start | bytes 6148
  1375.3 134.1 %copy-start.24 = (bf16[2,128,512]{2,1,0:T(8,128)(2,1)S(1)}, bf16[2,128,512]{2,1,0:T(8,128)(2,1)}, u32[]{:S(2)}) copy-start(bf16[2,128,512]{2,1,0:T(8,128)(2,1)} %param.23) | copy-start | bytes 786436
  1375.3 134.1 %all-gather.15.cloned.1.call-start = ((), (), s32[]{:S(2)}) async-start(), calls=%async_computation.33 | async-start | bytes 2949120 | tf_op jit(solution)/shard_map/all_gather | solution.py:71
  1448.0 134.1 %copy-start.47 = (f32[320]{0:T(512)S(1)}, f32[320]{0:T(512)}, u32[]{:S(2)}) copy-start(f32[320]{0:T(512)} %copy-done.46) | copy-start | bytes 3844
  1448.0 134.1 %copy-start.49 = (f32[320]{0:T(512)S(1)}, f32[320]{0:T(512)}, u32[]{:S(2)}) copy-start(f32[320]{0:T(512)} %copy-done.48) | copy-start | bytes 3844
  1448.0 134.1 %copy-start.67 = (f32[128]{0:T(128)S(1)}, f32[128]{0:T(128)}, u32[]{:S(2)}) copy-start(f32[128]{0:T(128)} %copy-done.66) | copy-start | bytes 1540
  1448.0 134.1 %copy-start.77 = (f32[128]{0:T(128)S(1)}, f32[128]{0:T(128)}, u32[]{:S(2)}) copy-start(f32[128]{0:T(128)} %copy-done.76) | copy-start | bytes 1540
  1448.0 182.5 %copy-start.39 = (bf16[2,128,128]{2,1,0:T(8,128)(2,1)S(1)}, bf16[2,128,128]{2,1,0:T(8,128)(2,1)}, u32[]{:S(2)}) copy-start(bf16[2,128,128]{2,1,0:T(8,128)(2,1)} %param.19) | copy-start | bytes 196612
  1448.0 134.1 %reduce-scatter.43.cloned.1.call-start = ((), (), s32[]{:S(2)}) async-start(), calls=%async_computation.34 | async-start | bytes 737280 | tf_op jit(solution)/shard_map/reduce_scatter | solution.py:118
  1512.8 119.2 %copy-start.63 = (f32[2,320]{1,0:T(2,128)S(1)}, f32[2,320]{1,0:T(2,128)}, u32[]{:S(2)}) copy-start(f32[2,320]{1,0:T(2,128)} %copy-done.62) | copy-start | bytes 7684
  1512.8 119.2 %copy-start.71 = (f32[2,320]{1,0:T(2,128)S(1)}, f32[2,320]{1,0:T(2,128)}, u32[]{:S(2)}) copy-start(f32[2,320]{1,0:T(2,128)} %copy-done.70) | copy-start | bytes 7684
  1512.8 162.6 %copy-start.36 = (bf16[320,128]{0,1:T(8,128)(2,1)S(1)}, bf16[320,128]{0,1:T(8,128)(2,1)}, u32[]{:S(2)}) copy-start(bf16[320,128]{0,1:T(8,128)(2,1)} %copy-done.35) | copy-start | bytes 245764
  1512.9 161.2 %reduce-scatter.45.cloned.1.call-start = ((), (), s32[]{:S(2)}) async-start(), calls=%async_computation.35 | async-start | bytes 737280 | tf_op jit(solution)/shard_map/reduce_scatter | solution.py:105
  1631.7 99.5 %all-gather.17.cloned.1.call-start = ((), (), s32[]{:S(2)}) async-start(), calls=%async_computation.36 | async-start | bytes 2211840 | tf_op jit(solution)/shard_map/all_gather | solution.py:71
  1677.8 81.5 %all-reduce.15.cloned.1.call-start = ((), (), s32[]{:S(2)}) async-start(), calls=%async_computation.39 | async-start | bytes 1572864 | tf_op jit(solution)/shard_map/psum | solution.py:336
  1688.5 46.2 %copy-start.31 = (bf16[1,128,3,128]{1,3,2,0:T(8,128)(2,1)S(1)}, bf16[1,128,3,128]{1,3,2,0:T(8,128)(2,1)}, u32[]{:S(2)}) copy-start(bf16[1,128,3,128]{1,3,2,0:T(8,128)(2,1)} %copy-done.30) | copy-start | bytes 294916
  1734.6 99.3 %copy-start.43 = (f32[320]{0:T(512)S(1)}, f32[320]{0:T(512)}, u32[]{:S(2)}) copy-start(f32[320]{0:T(512)} %copy-done.42) | copy-start | bytes 3844
  1734.6 99.3 %copy-start.45 = (f32[320]{0:T(512)S(1)}, f32[320]{0:T(512)}, u32[]{:S(2)}) copy-start(f32[320]{0:T(512)} %copy-done.44) | copy-start | bytes 3844
  1734.6 99.3 %copy-start.75 = (f32[128]{0:T(128)S(1)}, f32[128]{0:T(128)}, u32[]{:S(2)}) copy-start(f32[128]{0:T(128)} %copy-done.74) | copy-start | bytes 1540
  1734.6 99.3 %reduce-scatter.47.cloned.1.call-start = ((), (), s32[]{:S(2)}) async-start(), calls=%async_computation.37 | async-start | bytes 737280 | tf_op jit(solution)/shard_map/reduce_scatter | solution.py:118
  1736.2 258.1 %all-reduce.13.cloned.1.call-start = ((), (), s32[]{:S(2)}) async-start(), calls=%async_computation.38 | async-start | bytes 196608 | tf_op jit(solution)/shard_map/psum | solution.py:349
  1736.5 114.1 %copy-start.57 = (f32[2,1024]{1,0:T(2,128)}, f32[2,1024]{1,0:T(2,128)S(1)}, u32[]{:S(2)}) copy-start(f32[2,1024]{1,0:T(2,128)S(1)} %constant_dynamic-update-slice_fusion) | copy-start | bytes 24580
  1736.5 114.0 %copy-start.40 = (f32[2,4096]{1,0:T(2,128)}, f32[2,4096]{1,0:T(2,128)S(1)}, u32[]{:S(2)}) copy-start(f32[2,4096]{1,0:T(2,128)S(1)} %maximum_dynamic-update-slice_fusion) | copy-start | bytes 98308
  1736.6 114.0 %copy-start.58 = (f32[2,1024]{1,0:T(2,128)}, f32[2,1024]{1,0:T(2,128)S(1)}, u32[]{:S(2)}) copy-start(f32[2,1024]{1,0:T(2,128)S(1)} %constant_dynamic-update-slice_fusion.1) | copy-start | bytes 24580
  1736.6 113.9 %copy-start.59 = (f32[2,1024]{1,0:T(2,128)}, f32[2,1024]{1,0:T(2,128)S(1)}, u32[]{:S(2)}) copy-start(f32[2,1024]{1,0:T(2,128)S(1)} %constant_dynamic-update-slice_fusion.2) | copy-start | bytes 24580
  1736.7 113.9 %copy-start.60 = (f32[2,1024]{1,0:T(2,128)}, f32[2,1024]{1,0:T(2,128)S(1)}, u32[]{:S(2)}) copy-start(f32[2,1024]{1,0:T(2,128)S(1)} %constant_dynamic-update-slice_fusion.3) | copy-start | bytes 24580
  1736.9 113.7 %copy-start.41 = (f32[2,2,1024]{2,1,0:T(2,128)}, f32[2,2,1024]{2,1,0:T(2,128)S(1)}, u32[]{:S(2)}) copy-start(f32[2,2,1024]{2,1,0:T(2,128)S(1)} %constant_dynamic-update-slice_fusion.4) | copy-start | bytes 49156
  (51 other events, 517.0 us)
Sparse Core Ops, SparseCore 0:
  61.4 57.8 reduce-scatter.16
  149.4 73.1 reduce-scatter.18
  273.5 70.3 reduce-scatter.20
  347.2 61.2 all-gather.6
  412.4 69.0 reduce-scatter.22
  530.6 58.5 reduce-scatter.24
  624.1 74.3 reduce-scatter.26
  701.0 75.6 reduce-scatter.32
  779.1 61.6 reduce-scatter.28
  845.1 61.2 all-gather.10
  908.6 61.2 all-gather.8
  973.4 69.1 reduce-scatter.34
  1046.1 70.5 reduce-scatter.30
  1151.6 40.5 reduce-scatter.36
  1198.5 53.3 all-gather.12
  1255.3 68.8 reduce-scatter.38
  1375.4 70.4 reduce-scatter.40
  1448.1 61.2 all-gather.14
  1513.0 69.1 reduce-scatter.42
  1631.8 42.1 reduce-scatter.44
  1677.9 53.2 all-gather.16
  1734.7 24.5 all-reduce.14
  1763.3 70.5 reduce-scatter.46
  1851.3 143.0 all-reduce.12
where the time goes:
time: 2010 us
  waiting for transfers between devices  1440 us (72%)
  blocking collectives  419 us (21%)
  matrix products  56.7 us (3%)
  other arithmetic  42.8 us (2%)
  local copies, waits for them, and re-layouts  35.1 us (2%)
    reduce_scatter x4, waiting for transfers between devices, grad_token_sums(): lax.psum_scatter(partial_value(jnp.int32(0), lax.axis_size('col') * own_r...  275 us
    reduce_scatter x4, waiting for transfers between devices, head_sums(): lax.psum_scatter(partial_value(jnp.int32(0), lax.axis_size('row') * own_r...  250 us
    reduce_scatter x4, waiting for transfers between devices, token_sums(): lax.psum_scatter(partial_value(jnp.int32(0), lax.axis_size('col') * own_r...  237 us
    all_gather x4, waiting for transfers between devices, gather_grad_tokens(): return lax.all_gather(block, 'row', axis=0, tiled=True)  217 us
    reduce_scatter x4, waiting for transfers between devices, grad_head_sums(): lax.psum_scatter(partial_value(jnp.int32(0), lax.axis_size('row') * own_r...  175 us
    psum x1, waiting for transfers between devices, on_device(): summed = lax.psum(tuple(partials), ('dp', 'row', 'col'))  141 us
    all_gather x2, waiting for transfers between devices, gather_tokens(): return lax.all_gather(block, 'row', axis=0, tiled=True)  121 us
    all_gather x4, blocking collectives, gather_features(): return lax.all_gather(block, 'col', axis=0, tiled=True)  120 us
  transfers between devices with their start and end apart: 24, of which 24 were waited for; matrix products, arithmetic and copies ran while one was open for 2% of the time, Pallas kernels for 0%

commit v1 on v0

v1 whole, which is shorter than its diff:
```python
import functools

import jax
import jax.numpy as jnp
from jax import lax
from jax.experimental import pallas as pl
from jax.experimental.pallas import tpu as pltpu
from jax.sharding import PartitionSpec as P

BF = jnp.bfloat16
F32 = jnp.float32
LAYERS = 2
GROUP = 8
TOK = 40
SEQ = 320
D = 1024
HALF = 512
HEAD_DIM = 64
EPS = 1e-6
ROOT_HALF = 0.7071067811865476
INV_ROOT_TAU = 0.3989422804014327
MESH = pl.DeviceIdType.MESH


def dot(a, b):
    return jnp.dot(a, b, preferred_element_type=F32)


def dot_last(a, b):
    return lax.dot_general(a, b, (((1,), (1,)), ((), ())), preferred_element_type=F32)


def dot_first(a, b):
    return lax.dot_general(a, b, (((0,), (0,)), ((), ())), preferred_element_type=F32)


def lanes(parts):
    return jnp.concatenate(parts, axis=1)


def kernel(
    images, gain1, bias1, wqkv, qvb, wout, outb, gain2, bias2, wup, upb, wdown, downb, cot,
    enc_o, gin_o, gqkv_o, gout_o, gup_o, gdown_o, gg1_o, gb1_o, gqv_o, gob_o, gg2_o, gb2_o, gub_o, gdb_o,
    in_f, in_r, out_f, out_r,
    vec_s, vec_g, wq_g, wo_g, wu_g, wd_g,
    ag, rs_s, rs_r,
    gq_s, go_s, gu_s, gd_s, gq_r, go_r, gu_r, gd_r, sq, so, su, sd, tq, to, tu, td,
    stream, normal_k, scale_k, prob_k, qkv_k, mixed_k, hidden_k, slope_k, grad_k,
    vacc, vcol, vs_s, vs_r, vb_s, vb_r, vt_s, vt_r, vfin,
    in_ss, in_rs, out_ss, out_rs, vec_sem, w_ss, w_rs, ag_ss, ag_rs, rs_ss, rs_rs, g_ss, g_rs, x_ss, x_rs, v_ss, v_rs,
):
    core = lax.axis_index("dp")
    row = lax.axis_index("row")
    col = lax.axis_index("col")
    x = lax.div(col, 2)
    yh = lax.rem(col, 2)
    t = 2 * x + core

    def group_dev(j):
        return (lax.rem(j, 2), row, 2 * lax.div(j, 2) + yh)

    def plane_dev(r):
        return (yh, r, 2 * x + core)

    def push(src, dst, ssem, rsem, dev):
        pltpu.make_async_remote_copy(
            src_ref=src, dst_ref=dst, send_sem=ssem, recv_sem=rsem, device_id=dev, device_id_type=MESH
        ).start()

    def drain(ref, sem):
        pltpu.make_async_copy(ref, ref, sem).wait()

    def fan(me, own, src, dst, ssem, rsem, dev):
        @pl.when(own)
        def _():
            pltpu.make_async_copy(src(me), dst, rsem).start()

        @pl.when(jnp.logical_not(own))
        def _():
            push(src(me), dst, ssem, rsem, dev(me))

        @pl.loop(1, GROUP)
        def _(k):
            j = lax.rem(me + k, GROUP)
            push(src(j), dst, ssem, rsem, dev(j))

    def fan_sent(own, ref, ssem):
        @pl.when(own)
        def _():
            drain(ref.at[pl.ds(0, GROUP - 1)], ssem)

        @pl.when(jnp.logical_not(own))
        def _():
            drain(ref, ssem)

    own_plane = yh == core
    own_tile = jnp.logical_and(row == col, yh == core)

    in_f[0] = images[...].astype(F32).reshape(GROUP, TOK, 128)
    in_f[1] = cot[...].astype(F32).reshape(GROUP, TOK, 128)

    def tile_dev(j):
        return (lax.rem(j, 2), col, 2 * lax.div(j, 2) + core)

    def tiles_in(n):
        fan(t, own_tile, lambda j: in_f.at[n, j], in_r.at[n, row], in_ss.at[n], in_rs.at[n], tile_dev)

    tiles_in(0)

    vec_s[...] = jnp.zeros_like(vec_s)
    for l in range(LAYERS):
        for i, ref in enumerate((gain1, bias1, outb, gain2, bias2, downb)):
            vec_s[l, i : i + 1, :] = ref[l : l + 1, :]
        vec_s[2 + l, 0:2, :] = qvb[l]
        for j in range(4):
            vec_s[2 + l, 2 + j : 3 + j, :] = upb[l : l + 1, 128 * j : 128 * j + 128]
    fan(row, own_plane, lambda j: vec_s, vec_g.at[row], vec_sem.at[0], vec_sem.at[1], plane_dev)

    weights = ((wqkv, wq_g), (wout, wo_g), (wup, wu_g), (wdown, wd_g))

    def weights_in(l):
        for m, (src, dst) in enumerate(weights):
            fan(row, own_plane, lambda j, src=src: src.at[l], dst.at[l, row], w_ss.at[l, m], w_rs.at[l, m], plane_dev)

    def weight_wait(l, m):
        drain(weights[m][1].at[l], w_rs.at[l, m])

    weights_in(0)
    tiles_in(1)

    def gather_start(l, s, value):
        folded = jnp.concatenate([value[:, :HALF], value[:, HALF:]], axis=0).astype(BF)
        ag[l, s, t] = folded

        @pl.loop(1, GROUP)
        def _(k):
            j = lax.rem(t + k, GROUP)
            push(ag.at[l, s, t], ag.at[l, s, t], ag_ss.at[l, s], ag_rs.at[l, s], group_dev(j))

    def gather_wait(l, s):
        drain(ag.at[l, s, pl.ds(0, GROUP - 1)], ag_rs.at[l, s])

    def gather_read(l, s):
        whole = ag[l, s].astype(F32)
        left = whole[:, :TOK].reshape(SEQ, HALF).astype(BF)
        right = whole[:, TOK:].reshape(SEQ, HALF).astype(BF)
        return left, right

    def scatter_start(l, s, left, right):
        both = jnp.concatenate([left.reshape(GROUP, TOK, HALF), right.reshape(GROUP, TOK, HALF)], axis=1)
        rs_s[l, s] = both.astype(BF)
        rs_r[l, s, t] = rs_s[l, s, t]

        @pl.loop(1, GROUP)
        def _(k):
            j = lax.rem(t + k, GROUP)
            push(rs_s.at[l, s, j], rs_r.at[l, s, t], rs_ss.at[l, s], rs_rs.at[l, s], group_dev(j))

    def scatter_wait(l, s):
        drain(rs_r.at[l, s, pl.ds(0, GROUP - 1)], rs_rs.at[l, s])
        total = jnp.sum(rs_r[l, s].astype(F32), axis=0)
        return lanes([total[:TOK], total[TOK:]])

    def vec_row(l, i):
        return lanes([vec_g[r, l, i : i + 1, :] for r in range(GROUP)])

    def norm_forward(l, s, value):
        center = jnp.mean(value, axis=1, keepdims=True)
        shifted = value - center
        scaled = lax.rsqrt(jnp.mean(shifted * shifted, axis=1, keepdims=True) + EPS)
        normal = shifted * scaled
        normal_k[l, s] = normal
        scale_k[l, s] = jnp.broadcast_to(scaled, (TOK, 128))
        return normal * vec_row(l, 3 * s) + vec_row(l, 3 * s + 1)

    def norm_backward(l, s, grad_out):
        normal = normal_k[l, s]
        scaled = scale_k[l, s][:, 0:1]
        vacc[l, 3 * s : 3 * s + 1, :] = jnp.sum(grad_out * normal, axis=0, keepdims=True)
        vacc[l, 3 * s + 1 : 3 * s + 2, :] = jnp.sum(grad_out, axis=0, keepdims=True)
        upstream = grad_out * vec_row(l, 3 * s)
        mean_part = jnp.mean(upstream, axis=1, keepdims=True)
        proj_part = jnp.mean(upstream * normal, axis=1, keepdims=True)
        return scaled * (upstream - mean_part - normal * proj_part)

    def qkv_half(l, h):
        return wq_g[l, 4 * h : 4 * h + 4].reshape(HALF, 384)

    def out_half(l, h):
        return lanes([wo_g[l, 4 * h + r] for r in range(4)])

    def up_half(l, h):
        return wu_g[l, 4 * h : 4 * h + 4].reshape(HALF, 512)

    def down_half(l, h):
        return lanes([wd_g[l, 4 * h + r] for r in range(4)])

    def head_mask(h):
        lane = lax.broadcasted_iota(jnp.int32, (SEQ, 128), 1)
        return (lane < HEAD_DIM) if h == 0 else (lane >= HEAD_DIM)

    def pick(pair):
        return jnp.where(head_mask(0), pair[0], pair[1])

    def only(h, value):
        return jnp.where(head_mask(h), value, jnp.zeros_like(value))

    drain(in_r.at[0], in_rs.at[0])
    drain(vec_g, vec_sem.at[1])
    stream[...] = lanes([in_r[0, r] for r in range(GROUP)])

    @pl.loop(0, LAYERS)
    def _(l):
        gather_start(l, 0, norm_forward(l, 0, stream[...]))

        @pl.when(l == 0)
        def _():
            weights_in(1)

        weight_wait(l, 0)
        gather_wait(l, 0)
        left, right = gather_read(l, 0)
        projected = dot(left, qkv_half(l, 0)) + dot(right, qkv_half(l, 1))
        shift = vec_g[0, 2 + l]
        query = (projected[:, :128] + shift[0:1]).astype(BF)
        keys = projected[:, 128:256].astype(BF)
        values = (projected[:, 256:] + shift[1:2]).astype(BF)
        qkv_k[l, 0] = query
        qkv_k[l, 1] = keys
        qkv_k[l, 2] = values
        mixed = []
        for h in range(2):
            scores = dot_last(only(h, query), keys) * HEAD_DIM ** -0.5
            raised = jnp.exp(scores - jnp.max(scores, axis=1, keepdims=True))
            probs = raised / jnp.sum(raised, axis=1, keepdims=True)
            prob_k[l, h] = probs
            mixed.append(dot(probs.astype(BF), values))
        mixed = pick(mixed).astype(BF)
        mixed_k[l] = mixed
        weight_wait(l, 1)
        scatter_start(l, 0, dot(mixed, out_half(l, 0)), dot(mixed, out_half(l, 1)))
        base = stream[...] + vec_row(l, 2)
        middle = base + scatter_wait(l, 0)
        stream[...] = middle
        gather_start(l, 1, norm_forward(l, 1, middle))
        weight_wait(l, 2)
        gather_wait(l, 1)
        left, right = gather_read(l, 1)
        before = dot(left, up_half(l, 0)) + dot(right, up_half(l, 1))
        shift = vec_g[0, 2 + l]
        before = before + lanes([shift[2 + j : 3 + j] for j in range(4)])
        phi = 0.5 * (1.0 + lax.erf(before * ROOT_HALF))
        hidden = (before * phi).astype(BF)
        hidden_k[l] = hidden
        weight_wait(l, 3)
        scatter_start(l, 1, dot(hidden, down_half(l, 0)), dot(hidden, down_half(l, 1)))
        slope_k[l] = phi + before * INV_ROOT_TAU * jnp.exp(-0.5 * before * before)
        base = stream[...] + vec_row(l, 5)
        stream[...] = base + scatter_wait(l, 1)

    def back_dev(r):
        return (yh, r, row)

    def tiles_out(n, value):
        for r in range(GROUP):
            out_f[n, r] = value[:, 128 * r : 128 * r + 128]
        fan(row, own_tile, lambda j: out_f.at[n, j], out_r.at[n, t], out_ss.at[n], out_rs.at[n], back_dev)

    tiles_out(0, stream[...])

    drain(in_r.at[1], in_rs.at[1])
    grad_k[...] = lanes([in_r[1, r] for r in range(GROUP)])
    vacc[...] = jnp.zeros_like(vacc)
    vcol[...] = jnp.zeros_like(vcol)

    grads = ((gq_s, gq_r, sq, tq), (go_s, go_r, so, to), (gu_s, gu_r, su, tu), (gd_s, gd_r, sd, td))

    def grads_out(l, m):
        src, dst = grads[m][:2]
        fan(row, own_plane, lambda j: src.at[l, j], dst.at[l, row], g_ss.at[l, m], g_rs.at[l, m], plane_dev)

    @pl.loop(0, LAYERS)
    def _(step):
        l = LAYERS - 1 - step
        branch2 = grad_k[...]
        gather_start(l, 2, branch2)
        vacc[l, 5:6, :] = jnp.sum(branch2.astype(BF).astype(F32), axis=0, keepdims=True)
        gather_wait(l, 2)
        left, right = gather_read(l, 2)
        hidden_grad = dot_last(left, down_half(l, 0)) + dot_last(right, down_half(l, 1))
        before_grad = (hidden_grad * slope_k[l]).astype(BF)
        scatter_start(l, 2, dot_last(before_grad, up_half(l, 0)), dot_last(before_grad, up_half(l, 1)))
        sums = jnp.sum(before_grad.astype(F32), axis=0, keepdims=True)
        for j in range(4):
            vcol[l, 2 + j : 3 + j, :] = sums[:, 128 * j : 128 * j + 128]
        for h, part in enumerate((left, right)):
            product = dot_first(hidden_k[l], part).astype(BF)
            for r in range(4):
                gd_s[l, 4 * h + r] = product[:, 128 * r : 128 * r + 128]
        grads_out(l, 3)
        for h, part in enumerate(gather_read(l, 1)):
            gu_s[l, 4 * h : 4 * h + 4] = dot_first(part, before_grad).astype(BF).reshape(4, 128, 512)
        grads_out(l, 2)
        grad_mid = grad_k[...] + norm_backward(l, 1, scatter_wait(l, 2))
        grad_k[...] = grad_mid
        gather_start(l, 3, grad_mid)
        vacc[l, 2:3, :] = jnp.sum(grad_mid.astype(BF).astype(F32), axis=0, keepdims=True)
        gather_wait(l, 3)
        left, right = gather_read(l, 3)
        mixed_grad = (dot_last(left, out_half(l, 0)) + dot_last(right, out_half(l, 1))).astype(BF)
        query = qkv_k[l, 0]
        keys = qkv_k[l, 1]
        values = qkv_k[l, 2]
        value_grads, query_grads, key_grads = [], [], []
        for h in range(2):
            probs = prob_k[l, h]
            probs_grad = dot_last(only(h, mixed_grad), values)
            inner = jnp.sum(probs * probs_grad, axis=1, keepdims=True)
            scores_grad = (probs * (probs_grad - inner)).astype(BF)
            value_grads.append(dot_first(probs.astype(BF), mixed_grad))
            query_grads.append(dot(scores_grad, keys))
            key_grads.append(dot_first(scores_grad, query))
        query_grad = (pick(query_grads) * HEAD_DIM ** -0.5).astype(BF)
        keys_grad = (pick(key_grads) * HEAD_DIM ** -0.5).astype(BF)
        values_grad = pick(value_grads).astype(BF)
        joined = lanes([query_grad, keys_grad, values_grad])
        scatter_start(l, 3, dot_last(joined, qkv_half(l, 0)), dot_last(joined, qkv_half(l, 1)))
        vcol[l, 0:1, :] = jnp.sum(query_grad.astype(F32), axis=0, keepdims=True)
        vcol[l, 1:2, :] = jnp.sum(values_grad.astype(F32), axis=0, keepdims=True)
        for h, part in enumerate(gather_read(l, 0)):
            gq_s[l, 4 * h : 4 * h + 4] = dot_first(part, joined).astype(BF).reshape(4, 128, 384)
        grads_out(l, 0)
        for h, part in enumerate((left, right)):
            product = dot_first(mixed_k[l], part).astype(BF)
            for r in range(4):
                go_s[l, 4 * h + r] = product[:, 128 * r : 128 * r + 128]
        grads_out(l, 1)
        grad_k[...] = grad_k[...] + norm_backward(l, 0, scatter_wait(l, 3))

    tiles_out(1, grad_k[...])

    for j in range(GROUP):
        vs_s[j] = vacc[:, :, 128 * j : 128 * j + 128]
    vs_r[t] = vs_s[t]

    @pl.loop(1, GROUP)
    def _(k):
        j = lax.rem(t + k, GROUP)
        push(vs_s.at[j], vs_r.at[t], v_ss.at[0], v_rs.at[0], group_dev(j))

    sibling = (1 - core, row, col)

    def sum_terms(l):
        for m in (3, 2, 1, 0):
            src, dst, part, other = grads[m]
            drain(dst.at[l], g_rs.at[l, m])
            total = dst[l, 0].astype(F32)
            for r in range(1, GROUP):
                total += dst[l, r].astype(F32)
            part[l] = total
            push(part.at[l], other.at[l], x_ss.at[l, m], x_rs.at[l, m], sibling)

    sum_terms(1)

    drain(vs_r.at[pl.ds(0, GROUP - 1)], v_rs.at[0])
    vb_s[0:2] = jnp.sum(vs_r[...], axis=0)
    vb_s[2:4] = vcol[...]
    fan(row, own_plane, lambda j: vb_s, vb_r.at[row], v_ss.at[1], v_rs.at[1], plane_dev)

    drain(out_r.at[0], out_rs.at[0])
    enc_o[...] = out_r[0].reshape(SEQ, 128).astype(BF)

    drain(vb_r, v_rs.at[1])
    vt_s[...] = jnp.sum(vb_r[...], axis=0)
    push(vt_s, vt_r, v_ss.at[2], v_rs.at[2], sibling)

    sum_terms(0)

    drain(vt_r, v_rs.at[2])
    vt_s_total = vt_s[...] + vt_r[...]

    @pl.when(row == col)
    def _():
        vfin[...] = vt_s_total[0:2]

        @pl.loop(1, GROUP)
        def _(k):
            push(vfin, vfin, v_ss.at[3], v_rs.at[3], (core, row, lax.rem(col + k, GROUP)))

    for l in range(LAYERS):
        gqv_o[l] = vt_s_total[2 + l, 0:2]
        for j in range(4):
            gub_o[l : l + 1, 128 * j : 128 * j + 128] = vt_s_total[2 + l, 2 + j : 3 + j]

    drain(out_r.at[1], out_rs.at[1])
    gin_o[...] = out_r[1].reshape(SEQ, 128)

    @pl.when(row != col)
    def _():
        drain(vfin, v_rs.at[3])

    for l in range(LAYERS):
        for i, ref in enumerate((gg1_o, gb1_o, gob_o, gg2_o, gb2_o, gdb_o)):
            ref[l : l + 1, :] = vfin[l, i : i + 1, :]

    for l in (1, 0):
        for m, ref in ((3, gdown_o), (2, gup_o), (1, gout_o), (0, gqkv_o)):
            part, other = grads[m][2:]
            drain(other.at[l], x_rs.at[l, m])
            ref[l] = part[l] + other[l]

    for n in range(2):
        fan_sent(own_tile, in_f.at[n], in_ss.at[n])
        fan_sent(own_tile, out_f.at[n], out_ss.at[n])
    fan_sent(own_plane, vec_g, vec_sem.at[0])
    fan_sent(own_plane, vb_r, v_ss.at[1])
    drain(vs_s.at[pl.ds(0, GROUP - 1)], v_ss.at[0])
    drain(vt_s, v_ss.at[2])

    @pl.when(row == col)
    def _():
        drain(vs_r.at[pl.ds(0, GROUP - 1)], v_ss.at[3])

    @pl.loop(0, LAYERS)
    def _(l):
        for m in range(4):
            fan_sent(own_plane, weights[m][1].at[l], w_ss.at[l, m])
            fan_sent(own_plane, grads[m][0].at[l], g_ss.at[l, m])
            drain(grads[m][2].at[l], x_ss.at[l, m])
        for s in range(4):
            drain(ag.at[l, s, pl.ds(0, GROUP - 1)], ag_ss.at[l, s])
            drain(rs_s.at[l, s, pl.ds(0, GROUP - 1)], rs_ss.at[l, s])


def on_device(images, gain1, bias1, wqkv, qvb, wout, outb, gain2, bias2, wup, upb, wdown, downb, cot):
    L = LAYERS
    wqkv = wqkv.reshape(L, 128, 384)
    vmem = pl.BlockSpec(memory_space=pltpu.VMEM)
    shape = jax.ShapeDtypeStruct
    dma = pltpu.SemaphoreType.DMA
    V = pltpu.VMEM
    results = pl.pallas_call(
        kernel,
        out_shape=(
            shape((SEQ, 128), BF),
            shape((SEQ, 128), F32),
            shape((L, 128, 384), F32),
            shape((L, 128, 128), F32),
            shape((L, 128, 512), F32),
            shape((L, 512, 128), F32),
            shape((L, 128), F32),
            shape((L, 128), F32),
            shape((L, 2, 128), F32),
            shape((L, 128), F32),
            shape((L, 128), F32),
            shape((L, 128), F32),
            shape((L, 512), F32),
            shape((L, 128), F32),
        ),
        in_specs=[vmem] * 14,
        out_specs=(vmem,) * 14,
        scratch_shapes=[
            V((2, 8, TOK, 128), F32), V((2, 8, TOK, 128), F32), V((2, 8, TOK, 128), F32), V((2, 8, TOK, 128), F32),
            V((4, 8, 128), F32), V((8, 4, 8, 128), F32),
            V((L, 8, 128, 384), BF), V((L, 8, 128, 128), BF), V((L, 8, 128, 512), BF), V((L, 8, 512, 128), BF),
            V((L, 4, 8, 2 * TOK, HALF), BF), V((L, 4, 8, 2 * TOK, HALF), BF), V((L, 4, 8, 2 * TOK, HALF), BF),
            V((L, 8, 128, 384), BF), V((L, 8, 128, 128), BF), V((L, 8, 128, 512), BF), V((L, 8, 512, 128), BF),
            V((L, 8, 128, 384), BF), V((L, 8, 128, 128), BF), V((L, 8, 128, 512), BF), V((L, 8, 512, 128), BF),
            V((L, 128, 384), F32), V((L, 128, 128), F32), V((L, 128, 512), F32), V((L, 512, 128), F32),
            V((L, 128, 384), F32), V((L, 128, 128), F32), V((L, 128, 512), F32), V((L, 512, 128), F32),
            V((TOK, D), F32), V((L, 2, TOK, D), F32), V((L, 2, TOK, 128), F32), V((L, 2, SEQ, SEQ), F32),
            V((L, 3, SEQ, 128), BF), V((L, SEQ, 128), BF), V((L, SEQ, 512), BF), V((L, SEQ, 512), F32),
            V((TOK, D), F32),
            V((L, 8, D), F32), V((L, 8, 128), F32),
            V((8, L, 8, 128), F32), V((8, L, 8, 128), F32),
            V((4, 8, 128), F32), V((8, 4, 8, 128), F32),
            V((4, 8, 128), F32), V((4, 8, 128), F32), V((L, 8, 128), F32),
            dma((2,)), dma((2,)), dma((2,)), dma((2,)), dma((2,)),
            dma((L, 4)), dma((L, 4)), dma((L, 4)), dma((L, 4)), dma((L, 4)), dma((L, 4)),
            dma((L, 4)), dma((L, 4)), dma((L, 4)), dma((L, 4)), dma((4,)), dma((4,)),
        ],
        compiler_params=pltpu.CompilerParams(has_side_effects=True, vmem_limit_bytes=60 * 1024 * 1024),
        cost_estimate=pl.CostEstimate(flops=6 * 10**9, bytes_accessed=5 * 10**6, transcendentals=10**6),
    )(images, gain1, bias1, wqkv, qvb, wout, outb, gain2, bias2, wup, upb, wdown, downb, cot)
    results = list(results)
    results[2] = results[2].reshape(L, 128, 3, 128)
    return tuple(results)


def solution(mesh):
    return jax.shard_map(
        on_device,
        mesh=mesh,
        in_specs=(
            P(("dp", "col"), "row"),
            P(None, "row"),
            P(None, "row"),
            P(None, "row", None, "col"),
            P(None, None, "col"),
            P(None, "col", "row"),
            P(None, "row"),
            P(None, "row"),
            P(None, "row"),
            P(None, "row", "col"),
            P(None, "col"),
            P(None, "col", "row"),
            P(None, "row"),
            P(("dp", "col"), "row"),
        ),
        out_specs=(
            P(("dp", "col"), "row"),
            P(("dp", "col"), "row"),
            P(None, "row", None, "col"),
            P(None, "col", "row"),
            P(None, "row", "col"),
            P(None, "col", "row"),
            P(None, "row"),
            P(None, "row"),
            P(None, None, "col"),
            P(None, "row"),
            P(None, "row"),
            P(None, "row"),
            P(None, "col"),
            P(None, "row"),
        ),
        check_vma=False,
    )
```

time: 2010 us -> 229 us (0.11)
  waiting for transfers between devices: 1440 us -> 0 us
  blocking collectives: 419 us -> 0 us
  Pallas kernels: 0 us -> 213 us
  matrix products: 56.7 us -> 0 us
  other arithmetic: 42.8 us -> 0 us
  local copies, waits for them, and re-layouts: 35.1 us -> 12.7 us
    reduce_scatter x16 -> x0, waiting for transfers between devices: 937 us -> none  [the longest x4 275 us: grad_token_sums(): lax.psum_scatter(partial_value(jnp.int32(0), lax.axis_size('col') * own_r...]
    all_gather x6 -> x0, waiting for transfers between devices: 338 us -> none  [the longest x4 217 us: gather_grad_tokens(): return lax.all_gather(block, 'row', axis=0, tiled=True)]
    all_gather x10 -> x0, blocking collectives: 290 us -> none  [the longest x4 120 us: gather_features(): return lax.all_gather(block, 'col', axis=0, tiled=True)]
    pallas_call x0 -> x1, Pallas kernels: none -> 213 us  [on_device(): pl.pallas_call(kernel, out_shape=(shape((SEQ, 128), BF), shape((SEQ, 128)...]
    psum x2 -> x0, waiting for transfers between devices: 164 us -> none  [the longest x1 141 us: on_device(): summed = lax.psum(tuple(partials), ('dp', 'row', 'col'))]
    psum x8 -> x0, blocking collectives: 129 us -> none  [the longest x4 66.3 us: norm_forward(): lax.psum((jnp.sum(resid, axis=1), jnp.sum(resid * resid, axis=1)), 'row')]
    dot_general x36 -> x0, matrix products: 56.7 us -> none  [the longest x8 19.5 us: contract_last(): lax.dot_general(left, right, (((1,), (1,)), ((), ())), preferred_element_...]
    reduce_sum x15 -> x0, other arithmetic: 21.5 us -> none  [the longest x2 6.29 us: on_device(): up_shift_grad = jnp.sum(before_grad.astype(jnp.float32), axis=0)]
  transfers between devices with their start and end apart: 24 -> 0, of which waited for: 24 -> 0; matrix products, arithmetic and copies ran while one was open for 2% -> 0% of each run, Pallas kernels for 0% -> 0%
where the time goes in v1:
time: 229 us; the launch traced here: 227 us
  Pallas kernels  213 us (93%)
  local copies, waits for them, and re-layouts  12.7 us (6%)
    pallas_call x1, Pallas kernels, on_device(): pl.pallas_call(kernel, out_shape=(shape((SEQ, 128), BF), shape((SEQ, 128)...  213 us
    unnamed x41, local copies, waits for them, and re-layouts  10.7 us

profile of v1, /device:TPU:1, one launch (start us, length us, event | category | flops | bytes accessed | tf_op | source)
XLA Modules:
  0.0 226.5 jit_solution(10366796346220905572)
XLA Ops:
  0.6 1.1 copy.30
  1.7 0.8 copy.31.wqkv
  2.6 213.1 %shard_map.245 = (bf16[320,128]{1,0:T(8,128)(2,1)}, f32[320,128]{1,0:T(8,128)}, f32[2,128,384]{2,1,0:T(8,128)}, f32[2,128,128]{2,1,0:T(8,128)}, f32[2,128,512]{2...) custom-call(bf16[320,128]{1,0:T(8,128)(2,1)} %images.1, ...), custom_call_target="tpu_custom_call" | custom-call | flops 6000000000 | bytes 5000000 | tf_op jit(solution)/shard_map/pallas_call | solution.py:442
  215.7 1.2 copy.32
  216.8 0.0 copy-start.4
  216.8 0.0 copy-start.2
  216.9 0.0 copy-start.3
  216.9 0.9 copy.33
  217.8 0.0 copy-done.4
  217.8 0.0 copy-start.1
  217.8 0.6 copy.47
  218.4 0.0 copy-done.2
  218.4 0.7 copy.48
  219.1 0.0 copy-done.3
  219.1 0.7 copy.49
  219.7 0.0 copy-done.1
  219.8 0.0 copy-start
  219.8 0.8 copy.50
  220.5 0.4 copy-done
  221.0 0.0 copy-start.12
  221.0 0.0 copy-start.11
  221.0 0.0 copy-start.9
  221.0 0.0 copy-start.8
  221.0 0.8 copy.51
  221.8 0.0 copy-done.12
  221.8 0.0 copy-start.6
  221.8 0.6 copy.52
  222.4 0.0 copy-done.11
  222.4 0.6 copy.53
  222.9 0.0 copy-done.6
  222.9 0.0 copy-start.10
  222.9 0.6 copy.54
  223.5 0.1 copy-done.10
  223.6 0.0 copy-start.5
  223.6 0.6 copy.55
  224.2 0.0 copy-done.9
  224.2 0.6 copy.56
  224.7 0.0 copy-done.8
  224.7 0.6 copy.57
  225.3 0.0 copy-done.5
  225.3 0.0 copy-start.7
  225.3 0.6 copy.58
  225.9 0.1 copy-done.7
  225.9 0.6 copy.59
Async XLA Ops:
  216.8 0.9 copy-start.4
  216.8 1.6 copy-start.2
  216.9 2.2 copy-start.3
  217.8 2.0 copy-start.1
  219.8 1.2 copy-start
  221.0 0.8 copy-start.12
  221.0 1.4 copy-start.11
  221.0 3.2 %copy-start.9 = (f32[2,128]{1,0:T(2,128)S(1)}, f32[2,128]{1,0:T(2,128)}, u32[]{:S(2)}) copy-start(f32[2,128]{1,0:T(2,128)} %get-tuple-element.94) | copy-start | bytes 3076
  221.0 3.7 %copy-start.8 = (f32[2,128]{1,0:T(2,128)S(1)}, f32[2,128]{1,0:T(2,128)}, u32[]{:S(2)}) copy-start(f32[2,128]{1,0:T(2,128)} %get-tuple-element.95) | copy-start | bytes 3076
  221.8 1.1 copy-start.6
  222.9 0.7 copy-start.10
  223.6 1.7 copy-start.5
  225.3 0.7 copy-start.7

commit v2 on v1

--- a/solution.py
+++ b/solution.py
@@ -39,15 +39,18 @@
 
 
 def kernel(
-    images, gain1, bias1, wqkv, qvb, wout, outb, gain2, bias2, wup, upb, wdown, downb, cot,
+    images_h, gain1_h, bias1_h, wqkv, qvb_h, wout, outb_h, gain2_h, bias2_h, wup, upb_h, wdown, downb_h, cot_h,
+    enc_h, gin_h, gqkv_h, gout_h, gup_h, gdown_h, gg1_h, gb1_h, gqv_h, gob_h, gg2_h, gb2_h, gub_h, gdb_h,
+    images, gain1, bias1, qvb, outb, gain2, bias2, upb, downb, cot,
     enc_o, gin_o, gqkv_o, gout_o, gup_o, gdown_o, gg1_o, gb1_o, gqv_o, gob_o, gg2_o, gb2_o, gub_o, gdb_o,
     in_f, in_r, out_f, out_r,
     vec_s, vec_g, wq_g, wo_g, wu_g, wd_g,
-    ag, rs_s, rs_r,
+    ag, rs_s, rs_b, rs_c, rs_r,
     gq_s, go_s, gu_s, gd_s, gq_r, go_r, gu_r, gd_r, sq, so, su, sd, tq, to, tu, td,
     stream, normal_k, scale_k, prob_k, qkv_k, mixed_k, hidden_k, slope_k, grad_k,
-    vacc, vcol, vs_s, vs_r, vb_s, vb_r, vt_s, vt_r, vfin,
-    in_ss, in_rs, out_ss, out_rs, vec_sem, w_ss, w_rs, ag_ss, ag_rs, rs_ss, rs_rs, g_ss, g_rs, x_ss, x_rs, v_ss, v_rs,
+    vacc, vcol, vs_s, vs_r, vh_r, vb_r, vt_s, vt_r,
+    op_sem, res_sem, in_ss, in_rs, out_ss, out_rs, vec_sem, w_ss, w_rs,
+    ag_ss, ag_rs, ag_fs, rs_bs, rs_br, rs_ss, rs_rs, g_ss, g_rs, x_ss, x_rs, v_ss, v_rs,
 ):
     core = lax.axis_index("dp")
     row = lax.axis_index("row")
@@ -55,9 +58,11 @@
     x = lax.div(col, 2)
     yh = lax.rem(col, 2)
     t = 2 * x + core
-
-    def group_dev(j):
-        return (lax.rem(j, 2), row, 2 * lax.div(j, 2) + yh)
+    u = 4 * core + x
+    sibling = (1 - core, row, col)
+
+    def chip_dev(c):
+        return (core, row, 2 * c + yh)
 
     def plane_dev(r):
         return (yh, r, 2 * x + core)
@@ -94,19 +99,34 @@
             drain(ref, ssem)
 
     own_plane = yh == core
-    own_tile = jnp.logical_and(row == col, yh == core)
-
-    in_f[0] = images[...].astype(F32).reshape(GROUP, TOK, 128)
-    in_f[1] = cot[...].astype(F32).reshape(GROUP, TOK, 128)
+    own_tile = row == t
+
+    small = (
+        (images_h, images), (gain1_h, gain1), (bias1_h, bias1), (outb_h, outb), (gain2_h, gain2), (bias2_h, bias2),
+        (downb_h, downb), (qvb_h, qvb), (upb_h, upb), (cot_h, cot),
+    )
+    fetches = [pltpu.make_async_copy(src, dst, op_sem.at[n]) for n, (src, dst) in enumerate(small)]
+    for fetch in fetches:
+        fetch.start()
 
     def tile_dev(j):
-        return (lax.rem(j, 2), col, 2 * lax.div(j, 2) + core)
-
-    def tiles_in(n):
-        fan(t, own_tile, lambda j: in_f.at[n, j], in_r.at[n, row], in_ss.at[n], in_rs.at[n], tile_dev)
-
-    tiles_in(0)
-
+        return (lax.div(j, 4), t, 2 * lax.rem(j, 4) + yh)
+
+    def tiles_in(n, ref):
+        in_f[n, :, 0:TOK] = ref[...].astype(F32).reshape(GROUP, TOK, 128).astype(BF)
+        fan(u, own_tile, lambda j: in_f.at[n, j], in_r.at[n, row], in_ss.at[n], in_rs.at[n], tile_dev)
+
+    def tiles_read(ref, n):
+        whole = ref[n].astype(F32)
+        return [whole[r, 0:TOK] for r in range(GROUP)]
+
+    in_f[...] = jnp.zeros_like(in_f)
+    out_f[...] = jnp.zeros_like(out_f)
+    fetches[0].wait()
+    tiles_in(0, images)
+
+    for fetch in fetches[1:9]:
+        fetch.wait()
     vec_s[...] = jnp.zeros_like(vec_s)
     for l in range(LAYERS):
         for i, ref in enumerate((gain1, bias1, outb, gain2, bias2, downb)):
@@ -126,39 +146,55 @@
         drain(weights[m][1].at[l], w_rs.at[l, m])
 
     weights_in(0)
-    tiles_in(1)
+    fetches[9].wait()
+    tiles_in(1, cot)
+
+    def chip_at(k):
+        return lax.rem(x + k, 4)
 
     def gather_start(l, s, value):
         folded = jnp.concatenate([value[:, :HALF], value[:, HALF:]], axis=0).astype(BF)
-        ag[l, s, t] = folded
-
-        @pl.loop(1, GROUP)
-        def _(k):
-            j = lax.rem(t + k, GROUP)
-            push(ag.at[l, s, t], ag.at[l, s, t], ag_ss.at[l, s], ag_rs.at[l, s], group_dev(j))
+        ag[l, s, core, x] = folded
+        mine = ag.at[l, s, core, x]
+        for k in (2, 1, 3):
+            push(mine, mine, ag_ss.at[l, s], ag_rs.at[l, s, k], chip_dev(chip_at(k)))
+        push(mine, mine, ag_fs.at[l, s], ag_rs.at[l, s, 0], sibling)
 
     def gather_wait(l, s):
-        drain(ag.at[l, s, pl.ds(0, GROUP - 1)], ag_rs.at[l, s])
+        for k in (1, 3, 2):
+            came = ag.at[l, s, core, chip_at(4 - k)]
+            drain(came, ag_rs.at[l, s, k])
+            push(came, came, ag_fs.at[l, s], ag_rs.at[l, s, 0], sibling)
+        drain(ag.at[l, s, 0], ag_rs.at[l, s, 0])
 
     def gather_read(l, s):
-        whole = ag[l, s].astype(F32)
+        whole = ag[l, s].astype(F32).reshape(GROUP, 2 * TOK, HALF)
         left = whole[:, :TOK].reshape(SEQ, HALF).astype(BF)
         right = whole[:, TOK:].reshape(SEQ, HALF).astype(BF)
         return left, right
 
     def scatter_start(l, s, left, right):
         both = jnp.concatenate([left.reshape(GROUP, TOK, HALF), right.reshape(GROUP, TOK, HALF)], axis=1)
-        rs_s[l, s] = both.astype(BF)
-        rs_r[l, s, t] = rs_s[l, s, t]
-
-        @pl.loop(1, GROUP)
-        def _(k):
-            j = lax.rem(t + k, GROUP)
-            push(rs_s.at[l, s, j], rs_r.at[l, s, t], rs_ss.at[l, s], rs_rs.at[l, s], group_dev(j))
+        rs_s[l, s] = both.astype(BF).reshape(2, 4, 2 * TOK, HALF)
+        for k in (2, 1, 3, 0):
+            c = chip_at(k)
+            push(rs_s.at[l, s, 1 - core, c], rs_b.at[l, s, c], rs_bs.at[l, s], rs_br.at[l, s, k], sibling)
+
+    def pair_sum(l, s, k):
+        c = chip_at(k)
+        drain(rs_b.at[l, s, c], rs_br.at[l, s, k])
+        return rs_s[l, s, core, c].astype(F32) + rs_b[l, s, c].astype(F32)
+
+    def scatter_relay(l, s):
+        for k in (2, 1, 3):
+            rs_c[l, s, k] = pair_sum(l, s, k).astype(BF)
+            push(rs_c.at[l, s, k], rs_r.at[l, s, k], rs_ss.at[l, s], rs_rs.at[l, s, k], chip_dev(chip_at(k)))
 
     def scatter_wait(l, s):
-        drain(rs_r.at[l, s, pl.ds(0, GROUP - 1)], rs_rs.at[l, s])
-        total = jnp.sum(rs_r[l, s].astype(F32), axis=0)
+        total = pair_sum(l, s, 0)
+        for k in (1, 3, 2):
+            drain(rs_r.at[l, s, k], rs_rs.at[l, s, k])
+            total += rs_r[l, s, k].astype(F32)
         return lanes([total[:TOK], total[TOK:]])
 
     def vec_row(l, i):
@@ -184,7 +220,7 @@
         return scaled * (upstream - mean_part - normal * proj_part)
 
     def qkv_half(l, h):
-        return wq_g[l, 4 * h : 4 * h + 4].reshape(HALF, 384)
+        return jnp.concatenate([lanes([wq_g[l, 4 * h + r, j] for j in range(3)]) for r in range(4)], axis=0)
 
     def out_half(l, h):
         return lanes([wo_g[l, 4 * h + r] for r in range(4)])
@@ -206,8 +242,8 @@
         return jnp.where(head_mask(h), value, jnp.zeros_like(value))
 
     drain(in_r.at[0], in_rs.at[0])
+    stream[...] = lanes(tiles_read(in_r, 0))
     drain(vec_g, vec_sem.at[1])
-    stream[...] = lanes([in_r[0, r] for r in range(GROUP)])
 
     @pl.loop(0, LAYERS)
     def _(l):
@@ -217,9 +253,9 @@
         def _():
             weights_in(1)
 
-        weight_wait(l, 0)
         gather_wait(l, 0)
         left, right = gather_read(l, 0)
+        weight_wait(l, 0)
         projected = dot(left, qkv_half(l, 0)) + dot(right, qkv_half(l, 1))
         shift = vec_g[0, 2 + l]
         query = (projected[:, :128] + shift[0:1]).astype(BF)
@@ -239,13 +275,14 @@
         mixed_k[l] = mixed
         weight_wait(l, 1)
         scatter_start(l, 0, dot(mixed, out_half(l, 0)), dot(mixed, out_half(l, 1)))
+        scatter_relay(l, 0)
         base = stream[...] + vec_row(l, 2)
         middle = base + scatter_wait(l, 0)
         stream[...] = middle
         gather_start(l, 1, norm_forward(l, 1, middle))
-        weight_wait(l, 2)
         gather_wait(l, 1)
         left, right = gather_read(l, 1)
+        weight_wait(l, 2)
         before = dot(left, up_half(l, 0)) + dot(right, up_half(l, 1))
         shift = vec_g[0, 2 + l]
         before = before + lanes([shift[2 + j : 3 + j] for j in range(4)])
@@ -254,30 +291,43 @@
         hidden_k[l] = hidden
         weight_wait(l, 3)
         scatter_start(l, 1, dot(hidden, down_half(l, 0)), dot(hidden, down_half(l, 1)))
+        scatter_relay(l, 1)
         slope_k[l] = phi + before * INV_ROOT_TAU * jnp.exp(-0.5 * before * before)
         base = stream[...] + vec_row(l, 5)
         stream[...] = base + scatter_wait(l, 1)
 
     def back_dev(r):
-        return (yh, r, row)
+        return (lax.rem(row, 2), r, 2 * lax.div(row, 2) + yh)
 
     def tiles_out(n, value):
         for r in range(GROUP):
-            out_f[n, r] = value[:, 128 * r : 128 * r + 128]
-        fan(row, own_tile, lambda j: out_f.at[n, j], out_r.at[n, t], out_ss.at[n], out_rs.at[n], back_dev)
+            out_f[n, r, 0:TOK] = value[:, 128 * r : 128 * r + 128].astype(BF)
+        fan(row, own_tile, lambda j: out_f.at[n, j], out_r.at[n, u], out_ss.at[n], out_rs.at[n], back_dev)
 
     tiles_out(0, stream[...])
 
     drain(in_r.at[1], in_rs.at[1])
-    grad_k[...] = lanes([in_r[1, r] for r in range(GROUP)])
+    grad_k[...] = lanes(tiles_read(in_r, 1))
     vacc[...] = jnp.zeros_like(vacc)
     vcol[...] = jnp.zeros_like(vcol)
 
-    grads = ((gq_s, gq_r, sq, tq), (go_s, go_r, so, to), (gu_s, gu_r, su, tu), (gd_s, gd_r, sd, td))
+    grads = (
+        (gq_s, gq_r, sq, tq, gqkv_o, gqkv_h), (go_s, go_r, so, to, gout_o, gout_h),
+        (gu_s, gu_r, su, tu, gup_o, gup_h), (gd_s, gd_r, sd, td, gdown_o, gdown_h),
+    )
 
     def grads_out(l, m):
         src, dst = grads[m][:2]
         fan(row, own_plane, lambda j: src.at[l, j], dst.at[l, row], g_ss.at[l, m], g_rs.at[l, m], plane_dev)
+
+    def sum_terms(l, m):
+        src, dst, part, other = grads[m][:4]
+        drain(dst.at[l], g_rs.at[l, m])
+        total = dst[l, 0].astype(F32)
+        for r in range(1, GROUP):
+            total += dst[l, r].astype(F32)
+        part[l] = total
+        push(part.at[l], other.at[l], x_ss.at[l, m], x_rs.at[l, m], sibling)
 
     @pl.loop(0, LAYERS)
     def _(step):
@@ -293,6 +343,7 @@
         sums = jnp.sum(before_grad.astype(F32), axis=0, keepdims=True)
         for j in range(4):
             vcol[l, 2 + j : 3 + j, :] = sums[:, 128 * j : 128 * j + 128]
+        scatter_relay(l, 2)
         for h, part in enumerate((left, right)):
             product = dot_first(hidden_k[l], part).astype(BF)
             for r in range(4):
@@ -327,99 +378,100 @@
         scatter_start(l, 3, dot_last(joined, qkv_half(l, 0)), dot_last(joined, qkv_half(l, 1)))
         vcol[l, 0:1, :] = jnp.sum(query_grad.astype(F32), axis=0, keepdims=True)
         vcol[l, 1:2, :] = jnp.sum(values_grad.astype(F32), axis=0, keepdims=True)
+        scatter_relay(l, 3)
         for h, part in enumerate(gather_read(l, 0)):
-            gq_s[l, 4 * h : 4 * h + 4] = dot_first(part, joined).astype(BF).reshape(4, 128, 384)
+            product = dot_first(part, joined).astype(BF)
+            for r in range(4):
+                for j in range(3):
+                    gq_s[l, 4 * h + r, j] = product[128 * r : 128 * r + 128, 128 * j : 128 * j + 128]
         grads_out(l, 0)
         for h, part in enumerate((left, right)):
             product = dot_first(mixed_k[l], part).astype(BF)
             for r in range(4):
                 go_s[l, 4 * h + r] = product[:, 128 * r : 128 * r + 128]
         grads_out(l, 1)
+
+        @pl.when(l == 0)
+        def _():
+            fan(row, own_plane, lambda j: vcol, vb_r.at[row], v_ss.at[1], v_rs.at[1], plane_dev)
+            for m in (3, 2, 0, 1):
+                sum_terms(1, m)
+
         grad_k[...] = grad_k[...] + norm_backward(l, 0, scatter_wait(l, 3))
 
     tiles_out(1, grad_k[...])
 
     for j in range(GROUP):
         vs_s[j] = vacc[:, :, 128 * j : 128 * j + 128]
-    vs_r[t] = vs_s[t]
-
-    @pl.loop(1, GROUP)
-    def _(k):
-        j = lax.rem(t + k, GROUP)
-        push(vs_s.at[j], vs_r.at[t], v_ss.at[0], v_rs.at[0], group_dev(j))
-
-    sibling = (1 - core, row, col)
-
-    def sum_terms(l):
-        for m in (3, 2, 1, 0):
-            src, dst, part, other = grads[m]
-            drain(dst.at[l], g_rs.at[l, m])
-            total = dst[l, 0].astype(F32)
-            for r in range(1, GROUP):
-                total += dst[l, r].astype(F32)
-            part[l] = total
-            push(part.at[l], other.at[l], x_ss.at[l, m], x_rs.at[l, m], sibling)
-
-    sum_terms(1)
-
-    drain(vs_r.at[pl.ds(0, GROUP - 1)], v_rs.at[0])
-    vb_s[0:2] = jnp.sum(vs_r[...], axis=0)
-    vb_s[2:4] = vcol[...]
-    fan(row, own_plane, lambda j: vb_s, vb_r.at[row], v_ss.at[1], v_rs.at[1], plane_dev)
+    fan(row, own_plane, lambda j: vs_s.at[j], vs_r.at[row], v_ss.at[0], v_rs.at[0], plane_dev)
+
+    results = []
+
+    def result(src, dst):
+        copy = pltpu.make_async_copy(src, dst, res_sem.at[len(results)])
+        copy.start()
+        results.append(copy)
 
     drain(out_r.at[0], out_rs.at[0])
-    enc_o[...] = out_r[0].reshape(SEQ, 128).astype(BF)
+    enc_o[...] = out_r[0].astype(F32)[:, 0:TOK].reshape(SEQ, 128).astype(BF)
+    result(enc_o, enc_h)
 
     drain(vb_r, v_rs.at[1])
     vt_s[...] = jnp.sum(vb_r[...], axis=0)
     push(vt_s, vt_r, v_ss.at[2], v_rs.at[2], sibling)
 
-    sum_terms(0)
+    for m in (3, 2):
+        sum_terms(0, m)
+
+    drain(vs_r, v_rs.at[0])
+    place = 2 * col + core
+    vh_r[place] = jnp.sum(vs_r[...], axis=0)
+
+    @pl.loop(1, 2 * GROUP)
+    def _(k):
+        j = lax.rem(place + k, 2 * GROUP)
+        push(vh_r.at[place], vh_r.at[place], v_ss.at[3], v_rs.at[3], (lax.rem(j, 2), row, lax.div(j, 2)))
+
+    for m in (0, 1):
+        sum_terms(0, m)
 
     drain(vt_r, v_rs.at[2])
-    vt_s_total = vt_s[...] + vt_r[...]
-
-    @pl.when(row == col)
-    def _():
-        vfin[...] = vt_s_total[0:2]
-
-        @pl.loop(1, GROUP)
-        def _(k):
-            push(vfin, vfin, v_ss.at[3], v_rs.at[3], (core, row, lax.rem(col + k, GROUP)))
-
+    columns = vt_s[...] + vt_r[...]
     for l in range(LAYERS):
-        gqv_o[l] = vt_s_total[2 + l, 0:2]
+        gqv_o[l] = columns[l, 0:2]
         for j in range(4):
-            gub_o[l : l + 1, 128 * j : 128 * j + 128] = vt_s_total[2 + l, 2 + j : 3 + j]
+            gub_o[l : l + 1, 128 * j : 128 * j + 128] = columns[l, 2 + j : 3 + j]
+    result(gqv_o, gqv_h)
+    result(gub_o, gub_h)
 
     drain(out_r.at[1], out_rs.at[1])
-    gin_o[...] = out_r[1].reshape(SEQ, 128)
-
-    @pl.when(row != col)
-    def _():
-        drain(vfin, v_rs.at[3])
-
-    for l in range(LAYERS):
-        for i, ref in enumerate((gg1_o, gb1_o, gob_o, gg2_o, gb2_o, gdb_o)):
-            ref[l : l + 1, :] = vfin[l, i : i + 1, :]
-
-    for l in (1, 0):
-        for m, ref in ((3, gdown_o), (2, gup_o), (1, gout_o), (0, gqkv_o)):
-            part, other = grads[m][2:]
+    gin_o[...] = out_r[1].astype(F32)[:, 0:TOK].reshape(SEQ, 128)
+    result(gin_o, gin_h)
+
+    for m in (3, 2, 0, 1):
+        part, other, out, out_hbm = grads[m][2:]
+        for l in (1, 0):
             drain(other.at[l], x_rs.at[l, m])
-            ref[l] = part[l] + other[l]
+            out[l] = part[l] + other[l]
+        result(out, out_hbm)
+
+    drain(vh_r.at[pl.ds(0, 2 * GROUP - 1)], v_rs.at[3])
+    rows = jnp.sum(vh_r[...], axis=0)
+    for i, (ref, out_hbm) in enumerate(
+        ((gg1_o, gg1_h), (gb1_o, gb1_h), (gob_o, gob_h), (gg2_o, gg2_h), (gb2_o, gb2_h), (gdb_o, gdb_h))
+    ):
+        for l in range(LAYERS):
+            ref[l : l + 1, :] = rows[l, i : i + 1, :]
+        result(ref, out_hbm)
 
     for n in range(2):
         fan_sent(own_tile, in_f.at[n], in_ss.at[n])
         fan_sent(own_tile, out_f.at[n], out_ss.at[n])
     fan_sent(own_plane, vec_g, vec_sem.at[0])
     fan_sent(own_plane, vb_r, v_ss.at[1])
-    drain(vs_s.at[pl.ds(0, GROUP - 1)], v_ss.at[0])
+    fan_sent(own_plane, vs_s, v_ss.at[0])
     drain(vt_s, v_ss.at[2])
-
-    @pl.when(row == col)
-    def _():
-        drain(vs_r.at[pl.ds(0, GROUP - 1)], v_ss.at[3])
+    drain(vh_r.at[pl.ds(0, 2 * GROUP - 1)], v_ss.at[3])
 
     @pl.loop(0, LAYERS)
     def _(l):
@@ -428,62 +480,87 @@
             fan_sent(own_plane, grads[m][0].at[l], g_ss.at[l, m])
             drain(grads[m][2].at[l], x_ss.at[l, m])
         for s in range(4):
-            drain(ag.at[l, s, pl.ds(0, GROUP - 1)], ag_ss.at[l, s])
-            drain(rs_s.at[l, s, pl.ds(0, GROUP - 1)], rs_ss.at[l, s])
+            drain(ag.at[l, s, 0, pl.ds(0, 3)], ag_ss.at[l, s])
+            drain(ag.at[l, s, 0], ag_fs.at[l, s])
+            drain(rs_b.at[l, s], rs_bs.at[l, s])
+            drain(rs_c.at[l, s, pl.ds(1, 3)], rs_ss.at[l, s])
+
+    for copy in results:
+        copy.wait()
+
+
+def finish(*refs):
+    count = len(refs) // 2
+    sems = refs[-1]
+    copies = [pltpu.make_async_copy(refs[n], refs[count + n], sems.at[n]) for n in range(count)]
+    for copy in copies:
+        copy.start()
+    for copy in copies:
+        copy.wait()
 
 
 def on_device(images, gain1, bias1, wqkv, qvb, wout, outb, gain2, bias2, wup, upb, wdown, downb, cot):
     L = LAYERS
-    wqkv = wqkv.reshape(L, 128, 384)
-    vmem = pl.BlockSpec(memory_space=pltpu.VMEM)
+    wqkv = wqkv.transpose(0, 2, 1, 3)
+    hbm = pl.BlockSpec(memory_space=pl.ANY)
     shape = jax.ShapeDtypeStruct
     dma = pltpu.SemaphoreType.DMA
     V = pltpu.VMEM
+    out_shape = (
+        shape((SEQ, 128), BF),
+        shape((SEQ, 128), F32),
+        shape((L, 3, 128, 128), F32),
+        shape((L, 128, 128), F32),
+        shape((L, 128, 512), F32),
+        shape((L, 512, 128), F32),
+        shape((L, 128), F32),
+        shape((L, 128), F32),
+        shape((L, 2, 128), F32),
+        shape((L, 128), F32),
+        shape((L, 128), F32),
+        shape((L, 128), F32),
+        shape((L, 512), F32),
+        shape((L, 128), F32),
+    )
+    operands = (images, gain1, bias1, wqkv, qvb, wout, outb, gain2, bias2, wup, upb, wdown, downb, cot)
+    staged = [V(a.shape, a.dtype) for a in (images, gain1, bias1, qvb, outb, gain2, bias2, upb, downb, cot)]
     results = pl.pallas_call(
         kernel,
-        out_shape=(
-            shape((SEQ, 128), BF),
-            shape((SEQ, 128), F32),
-            shape((L, 128, 384), F32),
-            shape((L, 128, 128), F32),
-            shape((L, 128, 512), F32),
-            shape((L, 512, 128), F32),
-            shape((L, 128), F32),
-            shape((L, 128), F32),
-            shape((L, 2, 128), F32),
-            shape((L, 128), F32),
-            shape((L, 128), F32),
-            shape((L, 128), F32),
-            shape((L, 512), F32),
-            shape((L, 128), F32),
-        ),
-        in_specs=[vmem] * 14,
-        out_specs=(vmem,) * 14,
-        scratch_shapes=[
-            V((2, 8, TOK, 128), F32), V((2, 8, TOK, 128), F32), V((2, 8, TOK, 128), F32), V((2, 8, TOK, 128), F32),
+        out_shape=out_shape,
+        in_specs=[hbm] * 14,
+        out_specs=(hbm,) * 14,
+        scratch_shapes=staged + [V(a.shape, a.dtype) for a in out_shape] + [
+            V((2, 8, 48, 128), BF), V((2, 8, 48, 128), BF), V((2, 8, 48, 128), BF), V((2, 8, 48, 128), BF),
             V((4, 8, 128), F32), V((8, 4, 8, 128), F32),
-            V((L, 8, 128, 384), BF), V((L, 8, 128, 128), BF), V((L, 8, 128, 512), BF), V((L, 8, 512, 128), BF),
-            V((L, 4, 8, 2 * TOK, HALF), BF), V((L, 4, 8, 2 * TOK, HALF), BF), V((L, 4, 8, 2 * TOK, HALF), BF),
-            V((L, 8, 128, 384), BF), V((L, 8, 128, 128), BF), V((L, 8, 128, 512), BF), V((L, 8, 512, 128), BF),
-            V((L, 8, 128, 384), BF), V((L, 8, 128, 128), BF), V((L, 8, 128, 512), BF), V((L, 8, 512, 128), BF),
-            V((L, 128, 384), F32), V((L, 128, 128), F32), V((L, 128, 512), F32), V((L, 512, 128), F32),
-            V((L, 128, 384), F32), V((L, 128, 128), F32), V((L, 128, 512), F32), V((L, 512, 128), F32),
+            V((L, 8, 3, 128, 128), BF), V((L, 8, 128, 128), BF), V((L, 8, 128, 512), BF), V((L, 8, 512, 128), BF),
+            V((L, 4, 2, 4, 2 * TOK, HALF), BF), V((L, 4, 2, 4, 2 * TOK, HALF), BF),
+            V((L, 4, 4, 2 * TOK, HALF), BF), V((L, 4, 4, 2 * TOK, HALF), BF), V((L, 4, 4, 2 * TOK, HALF), BF),
+            V((L, 8, 3, 128, 128), BF), V((L, 8, 128, 128), BF), V((L, 8, 128, 512), BF), V((L, 8, 512, 128), BF),
+            V((L, 8, 3, 128, 128), BF), V((L, 8, 128, 128), BF), V((L, 8, 128, 512), BF), V((L, 8, 512, 128), BF),
+            V((L, 3, 128, 128), F32), V((L, 128, 128), F32), V((L, 128, 512), F32), V((L, 512, 128), F32),
+            V((L, 3, 128, 128), F32), V((L, 128, 128), F32), V((L, 128, 512), F32), V((L, 512, 128), F32),
             V((TOK, D), F32), V((L, 2, TOK, D), F32), V((L, 2, TOK, 128), F32), V((L, 2, SEQ, SEQ), F32),
             V((L, 3, SEQ, 128), BF), V((L, SEQ, 128), BF), V((L, SEQ, 512), BF), V((L, SEQ, 512), F32),
             V((TOK, D), F32),
             V((L, 8, D), F32), V((L, 8, 128), F32),
-            V((8, L, 8, 128), F32), V((8, L, 8, 128), F32),
-            V((4, 8, 128), F32), V((8, 4, 8, 128), F32),
-            V((4, 8, 128), F32), V((4, 8, 128), F32), V((L, 8, 128), F32),
-            dma((2,)), dma((2,)), dma((2,)), dma((2,)), dma((2,)),
-            dma((L, 4)), dma((L, 4)), dma((L, 4)), dma((L, 4)), dma((L, 4)), dma((L, 4)),
+            V((8, L, 8, 128), F32), V((8, L, 8, 128), F32), V((16, L, 8, 128), F32),
+            V((8, L, 8, 128), F32), V((L, 8, 128), F32), V((L, 8, 128), F32),
+            dma((10,)), dma((14,)), dma((2,)), dma((2,)), dma((2,)), dma((2,)), dma((2,)), dma((L, 4)), dma((L, 4)),
+            dma((L, 4)), dma((L, 4, 4)), dma((L, 4)), dma((L, 4)), dma((L, 4, 4)), dma((L, 4)), dma((L, 4, 4)),
             dma((L, 4)), dma((L, 4)), dma((L, 4)), dma((L, 4)), dma((4,)), dma((4,)),
         ],
         compiler_params=pltpu.CompilerParams(has_side_effects=True, vmem_limit_bytes=60 * 1024 * 1024),
         cost_estimate=pl.CostEstimate(flops=6 * 10**9, bytes_accessed=5 * 10**6, transcendentals=10**6),
-    )(images, gain1, bias1, wqkv, qvb, wout, outb, gain2, bias2, wup, upb, wdown, downb, cot)
+    )(*operands)
+    results = pl.pallas_call(
+        finish,
+        out_shape=out_shape,
+        in_specs=[hbm] * 14,
+        out_specs=(hbm,) * 14,
+        scratch_shapes=[dma((14,))],
+    )(*results)
     results = list(results)
-    results[2] = results[2].reshape(L, 128, 3, 128)
+    results[2] = results[2].transpose(0, 2, 1, 3)
     return tuple(results)
 
 

time: 229 us -> 254 us (1.11); the launches traced: 227 us -> 254 us
  Pallas kernels: 213 us -> 254 us
  local copies, waits for them, and re-layouts: 12.7 us -> 0 us
    pallas_call x1 -> x2, Pallas kernels: 213 us -> 254 us  [the longest x1 197 us: on_device(): pl.pallas_call(kernel, out_shape=out_shape, in_specs=[hbm] * 14, out_spec...]
    unnamed x41 -> x0, local copies, waits for them, and re-layouts: 10.7 us -> none
where the time goes in v2:
time: 254 us
  Pallas kernels  254 us (100%)
    pallas_call x1, Pallas kernels, on_device(): pl.pallas_call(kernel, out_shape=out_shape, in_specs=[hbm] * 14, out_spec...  197 us
    pallas_call x1, Pallas kernels, on_device(): pl.pallas_call(finish, out_shape=out_shape, in_specs=[hbm] * 14, out_spec...  56.7 us

profile of v2, /device:TPU:1, one launch (start us, length us, event | category | flops | bytes accessed | tf_op | source)
XLA Modules:
  0.0 254.2 jit_solution(17150354056391437170)
XLA Ops:
  0.7 196.9 %shard_map.245 = (bf16[320,128]{1,0:T(8,128)(2,1)}, f32[320,128]{1,0:T(8,128)}, f32[2,3,128,128]{3,2,1,0:T(8,128)}, f32[2,128,128]{2,1,0:T(8,128)}, f32[2,128,51...) custom-call(bf16[320,128]{1,0:T(8,128)(2,1)} %images_h.1, ...), custom_call_target="tpu_custom_call" | custom-call | flops 6000000000 | bytes 5000000 | tf_op jit(solution)/shard_map/pallas_call | solution.py:527
  197.5 56.7 %shard_map.246 = (bf16[320,128]{1,0:T(8,128)(2,1)}, f32[320,128]{1,0:T(8,128)}, f32[2,3,128,128]{3,2,1,0:T(8,128)}, f32[2,128,128]{2,1,0:T(8,128)}, f32[2,128,51...) custom-call(bf16[320,128]{1,0:T(8,128)(2,1)} %get-tuple-element.42.r, ...), custom_call_target="tpu_custom_call" | custom-call | tf_op jit(solution)/shard_map/pallas_call | solution.py:555

commit v3 on v2

--- a/solution.py
+++ b/solution.py
@@ -46,17 +46,20 @@
     in_f, in_r, out_f, out_r,
     vec_s, vec_g, wq_g, wo_g, wu_g, wd_g,
     ag, rs_s, rs_b, rs_c, rs_r,
-    gq_s, go_s, gu_s, gd_s, gq_r, go_r, gu_r, gd_r, sq, so, su, sd, tq, to, tu, td,
+    gq_s, go_s, gu_s, gd_s, gq_r, go_r, gu_r, gd_r, gu_c, gu_f, gd_c, gd_f, sq, so, su, sd, tq, to, tu, td,
     stream, normal_k, scale_k, prob_k, qkv_k, mixed_k, hidden_k, slope_k, grad_k,
     vacc, vcol, vs_s, vs_r, vh_r, vb_r, vt_s, vt_r,
-    op_sem, res_sem, in_ss, in_rs, out_ss, out_rs, vec_sem, w_ss, w_rs,
-    ag_ss, ag_rs, ag_fs, rs_bs, rs_br, rs_ss, rs_rs, g_ss, g_rs, x_ss, x_rs, v_ss, v_rs,
+    op_sem, res_sem, in_ss, in_rs, out_ss, out_rs, vec_sem, w_ss, w_rs, wf_ss, wf_rs,
+    ag_ss, ag_rs, ag_fs, rs_bs, rs_br, rs_ss, rs_rs, g_ss, g_rs, gf_ss, gf_rs, x_ss, x_rs, v_ss, v_rs,
 ):
     core = lax.axis_index("dp")
     row = lax.axis_index("row")
     col = lax.axis_index("col")
     x = lax.div(col, 2)
     yh = lax.rem(col, 2)
+    z = lax.div(row, 2)
+    yl = lax.rem(row, 2)
+    y = 2 * yh + yl
     t = 2 * x + core
     u = 4 * core + x
     sibling = (1 - core, row, col)
@@ -100,6 +103,48 @@
 
     own_plane = yh == core
     own_tile = row == t
+    place = 2 * col + core
+
+    def tile_dev(j):
+        return (lax.div(j, 4), t, 2 * lax.rem(j, 4) + yh)
+
+    def back_dev(r):
+        return (lax.rem(row, 2), r, 2 * lax.div(row, 2) + yh)
+
+    def y_dev(k):
+        other = lax.rem(y + k, 4)
+        return (core, 2 * z + lax.rem(other, 2), 2 * x + lax.div(other, 2))
+
+    def z_at(k):
+        return lax.rem(z + k, 4)
+
+    def z_dev(k):
+        return (core, 2 * z_at(k) + yl, col)
+
+    def row_dev(j):
+        return (lax.rem(j, 2), row, lax.div(j, 2))
+
+    barrier = pltpu.get_barrier_semaphore()
+
+    def greet(me, own, dev):
+        @pl.when(jnp.logical_not(own))
+        def _():
+            pl.semaphore_signal(barrier, inc=1, device_id=dev(me), device_id_type=MESH)
+
+        @pl.loop(1, GROUP)
+        def _(k):
+            pl.semaphore_signal(barrier, inc=1, device_id=dev(lax.rem(me + k, GROUP)), device_id_type=MESH)
+
+    greet(u, own_tile, tile_dev)
+    greet(row, own_tile, back_dev)
+    greet(row, own_plane, plane_dev)
+    for k in (1, 2, 3):
+        pl.semaphore_signal(barrier, inc=1, device_id=y_dev(k), device_id_type=MESH)
+        pl.semaphore_signal(barrier, inc=1, device_id=z_dev(k), device_id_type=MESH)
+
+    @pl.loop(1, 2 * GROUP)
+    def _(k):
+        pl.semaphore_signal(barrier, inc=1, device_id=row_dev(lax.rem(place + k, 2 * GROUP)), device_id_type=MESH)
 
     small = (
         (images_h, images), (gain1_h, gain1), (bias1_h, bias1), (outb_h, outb), (gain2_h, gain2), (bias2_h, bias2),
@@ -109,11 +154,10 @@
     for fetch in fetches:
         fetch.start()
 
-    def tile_dev(j):
-        return (lax.div(j, 4), t, 2 * lax.rem(j, 4) + yh)
-
-    def tiles_in(n, ref):
+    def tiles_fold(n, ref):
         in_f[n, :, 0:TOK] = ref[...].astype(F32).reshape(GROUP, TOK, 128).astype(BF)
+
+    def tiles_in(n):
         fan(u, own_tile, lambda j: in_f.at[n, j], in_r.at[n, row], in_ss.at[n], in_rs.at[n], tile_dev)
 
     def tiles_read(ref, n):
@@ -123,7 +167,11 @@
     in_f[...] = jnp.zeros_like(in_f)
     out_f[...] = jnp.zeros_like(out_f)
     fetches[0].wait()
-    tiles_in(0, images)
+    tiles_fold(0, images)
+
+    greeted = 3 * GROUP + 6 + 2 * GROUP - 1
+    pl.semaphore_wait(barrier, greeted - jnp.where(own_plane, 1, 0) - jnp.where(own_tile, 2, 0))
+    tiles_in(0)
 
     for fetch in fetches[1:9]:
         fetch.wait()
@@ -138,16 +186,70 @@
 
     weights = ((wqkv, wq_g), (wout, wo_g), (wup, wu_g), (wdown, wd_g))
 
+    def y_first(m):
+        return m in (0, 3)
+
+    def weight_slot(m, r):
+        return r if y_first(m) else 4 * (r % 2) + r // 2
+
     def weights_in(l):
-        for m, (src, dst) in enumerate(weights):
-            fan(row, own_plane, lambda j, src=src: src.at[l], dst.at[l, row], w_ss.at[l, m], w_rs.at[l, m], plane_dev)
+        @pl.when(own_plane)
+        def _():
+            for m, (src, dst) in enumerate(weights):
+                block = dst.at[l, row if y_first(m) else 4 * yl + z]
+                pltpu.make_async_copy(src.at[l], block, w_rs.at[l, m]).start()
+                for k in (2, 1, 3):
+                    push(src.at[l], block, w_ss.at[l, m], w_rs.at[l, m], (y_dev if y_first(m) else z_dev)(k))
+
+    def weights_relay(l, m):
+        dst = weights[m][1]
+        if y_first(m):
+            pair = dst.at[l, pl.ds(2 * z, 2)]
+            drain(pair, w_rs.at[l, m])
+            for k in (2, 1, 3):
+                push(pair, pair, wf_ss.at[l, m], wf_rs.at[l, m], z_dev(k))
+        else:
+
+            @pl.when(own_plane)
+            def _():
+                four = dst.at[l, pl.ds(4 * yl, 4)]
+                drain(four, w_rs.at[l, m])
+                for k in (2, 1, 3):
+                    push(four, four, wf_ss.at[l, m], wf_rs.at[l, m], y_dev(k))
 
     def weight_wait(l, m):
-        drain(weights[m][1].at[l], w_rs.at[l, m])
+        dst = weights[m][1]
+        if y_first(m):
+            drain(dst.at[l, pl.ds(0, 6)], wf_rs.at[l, m])
+        else:
+
+            @pl.when(own_plane)
+            def _():
+                drain(dst.at[l, pl.ds(0, 4)], wf_rs.at[l, m])
+
+            @pl.when(jnp.logical_not(own_plane))
+            def _():
+                drain(dst.at[l], wf_rs.at[l, m])
+
+    def weights_sent(l, m):
+        dst = weights[m][1]
+
+        @pl.when(own_plane)
+        def _():
+            drain(dst.at[l, pl.ds(0, 3)], w_ss.at[l, m])
+
+        if y_first(m):
+            drain(dst.at[l, pl.ds(0, 6)], wf_ss.at[l, m])
+        else:
+
+            @pl.when(own_plane)
+            def _():
+                drain(dst.at[:, pl.ds(0, 6)], wf_ss.at[l, m])
 
     weights_in(0)
     fetches[9].wait()
-    tiles_in(1, cot)
+    tiles_fold(1, cot)
+    tiles_in(1)
 
     def chip_at(k):
         return lax.rem(x + k, 4)
@@ -220,16 +322,16 @@
         return scaled * (upstream - mean_part - normal * proj_part)
 
     def qkv_half(l, h):
-        return jnp.concatenate([lanes([wq_g[l, 4 * h + r, j] for j in range(3)]) for r in range(4)], axis=0)
+        return jnp.concatenate([lanes([wq_g[l, weight_slot(0, 4 * h + r), j] for j in range(3)]) for r in range(4)], axis=0)
 
     def out_half(l, h):
-        return lanes([wo_g[l, 4 * h + r] for r in range(4)])
+        return lanes([wo_g[l, weight_slot(1, 4 * h + r)] for r in range(4)])
 
     def up_half(l, h):
-        return wu_g[l, 4 * h : 4 * h + 4].reshape(HALF, 512)
+        return jnp.concatenate([wu_g[l, weight_slot(2, 4 * h + r)] for r in range(4)], axis=0)
 
     def down_half(l, h):
-        return lanes([wd_g[l, 4 * h + r] for r in range(4)])
+        return lanes([wd_g[l, weight_slot(3, 4 * h + r)] for r in range(4)])
 
     def head_mask(h):
         lane = lax.broadcasted_iota(jnp.int32, (SEQ, 128), 1)
@@ -251,7 +353,8 @@
 
         @pl.when(l == 0)
         def _():
-            weights_in(1)
+            for m in (0, 1, 2):
+                weights_relay(0, m)
 
         gather_wait(l, 0)
         left, right = gather_read(l, 0)
@@ -276,6 +379,12 @@
         weight_wait(l, 1)
         scatter_start(l, 0, dot(mixed, out_half(l, 0)), dot(mixed, out_half(l, 1)))
         scatter_relay(l, 0)
+
+        @pl.when(l == 0)
+        def _():
+            weights_relay(0, 3)
+            weights_in(1)
+
         base = stream[...] + vec_row(l, 2)
         middle = base + scatter_wait(l, 0)
         stream[...] = middle
@@ -292,12 +401,15 @@
         weight_wait(l, 3)
         scatter_start(l, 1, dot(hidden, down_half(l, 0)), dot(hidden, down_half(l, 1)))
         scatter_relay(l, 1)
+
+        @pl.when(l == 0)
+        def _():
+            for m in range(4):
+                weights_relay(1, m)
+
         slope_k[l] = phi + before * INV_ROOT_TAU * jnp.exp(-0.5 * before * before)
         base = stream[...] + vec_row(l, 5)
         stream[...] = base + scatter_wait(l, 1)
-
-    def back_dev(r):
-        return (lax.rem(row, 2), r, 2 * lax.div(row, 2) + yh)
 
     def tiles_out(n, value):
         for r in range(GROUP):
@@ -316,16 +428,84 @@
         (gu_s, gu_r, su, tu, gup_o, gup_h), (gd_s, gd_r, sd, td, gdown_o, gdown_h),
     )
 
+    def grad_slot(m, r):
+        return 4 * (r % 2) + r // 2 if m == 3 else r
+
+    def pair_fan(src, dst, ssem, rsem):
+        def dev(j):
+            return plane_dev(2 * z + j)
+
+        @pl.when(own_plane)
+        def _():
+            pltpu.make_async_copy(src(yl), dst, rsem).start()
+
+        @pl.when(jnp.logical_not(own_plane))
+        def _():
+            push(src(yl), dst, ssem, rsem, dev(yl))
+
+        push(src(1 - yl), dst, ssem, rsem, dev(1 - yl))
+
     def grads_out(l, m):
         src, dst = grads[m][:2]
-        fan(row, own_plane, lambda j: src.at[l, j], dst.at[l, row], g_ss.at[l, m], g_rs.at[l, m], plane_dev)
+        if m == 2:
+            for k in (2, 1, 3):
+                push(src.at[l, pl.ds(2 * z_at(k), 2)], dst.at[l, k], g_ss.at[l, m], g_rs.at[l, m], z_dev(k))
+        elif m == 3:
+            pair_fan(lambda j: src.at[l, pl.ds(4 * j, 4)], dst.at[l, yl], g_ss.at[l, m], g_rs.at[l, m])
+        else:
+            fan(row, own_plane, lambda j: src.at[l, j], dst.at[l, row], g_ss.at[l, m], g_rs.at[l, m], plane_dev)
+
+    def up_relay(l):
+        drain(gu_r.at[l, pl.ds(1, 3)], g_rs.at[l, 2])
+        for j in range(2):
+            total = gu_s[l, 2 * z + j].astype(F32)
+            for k in (1, 2, 3):
+                total += gu_r[l, k, j].astype(F32)
+            gu_c[l, j] = total.astype(BF)
+        pair_fan(lambda j: gu_c.at[l, j], gu_f.at[l, yl], gf_ss.at[l, 0], gf_rs.at[l, 0])
+
+    def down_relay(l):
+        drain(gd_r.at[l], g_rs.at[l, 3])
+        for j in range(4):
+            gd_c[l, j] = (gd_r[l, 0, j].astype(F32) + gd_r[l, 1, j].astype(F32)).astype(BF)
+        for k in (2, 1, 3):
+            push(gd_c.at[l, z_at(k)], gd_f.at[l, k], gf_ss.at[l, 1], gf_rs.at[l, 1], z_dev(k))
+
+    def pair_sent(ref, ssem):
+        @pl.when(own_plane)
+        def _():
+            drain(ref.at[0], ssem)
+
+        @pl.when(jnp.logical_not(own_plane))
+        def _():
+            drain(ref, ssem)
+
+    def grads_sent(l, m):
+        src, dst = grads[m][:2]
+        if m == 2:
+            drain(dst.at[l, pl.ds(1, 3)], g_ss.at[l, m])
+            pair_sent(gu_c.at[l], gf_ss.at[l, 0])
+        elif m == 3:
+            pair_sent(dst.at[l], g_ss.at[l, m])
+            drain(gd_f.at[l, pl.ds(1, 3)], gf_ss.at[l, 1])
+        else:
+            fan_sent(own_plane, src.at[l], g_ss.at[l, m])
 
     def sum_terms(l, m):
         src, dst, part, other = grads[m][:4]
-        drain(dst.at[l], g_rs.at[l, m])
-        total = dst[l, 0].astype(F32)
-        for r in range(1, GROUP):
-            total += dst[l, r].astype(F32)
+        if m == 2:
+            drain(gu_f.at[l], gf_rs.at[l, 0])
+            total = gu_f[l, 0].astype(F32) + gu_f[l, 1].astype(F32)
+        elif m == 3:
+            drain(gd_f.at[l, pl.ds(1, 3)], gf_rs.at[l, 1])
+            total = gd_c[l, z].astype(F32)
+            for k in (1, 2, 3):
+                total += gd_f[l, k].astype(F32)
+        else:
+            drain(dst.at[l], g_rs.at[l, m])
+            total = dst[l, 0].astype(F32)
+            for r in range(1, GROUP):
+                total += dst[l, r].astype(F32)
         part[l] = total
         push(part.at[l], other.at[l], x_ss.at[l, m], x_rs.at[l, m], sibling)
 
@@ -347,7 +527,7 @@
         for h, part in enumerate((left, right)):
             product = dot_first(hidden_k[l], part).astype(BF)
             for r in range(4):
-                gd_s[l, 4 * h + r] = product[:, 128 * r : 128 * r + 128]
+                gd_s[l, grad_slot(3, 4 * h + r)] = product[:, 128 * r : 128 * r + 128]
         grads_out(l, 3)
         for h, part in enumerate(gather_read(l, 1)):
             gu_s[l, 4 * h : 4 * h + 4] = dot_first(part, before_grad).astype(BF).reshape(4, 128, 512)
@@ -359,6 +539,11 @@
         gather_wait(l, 3)
         left, right = gather_read(l, 3)
         mixed_grad = (dot_last(left, out_half(l, 0)) + dot_last(right, out_half(l, 1))).astype(BF)
+        for h, part in enumerate((left, right)):
+            product = dot_first(mixed_k[l], part).astype(BF)
+            for r in range(4):
+                go_s[l, 4 * h + r] = product[:, 128 * r : 128 * r + 128]
+        grads_out(l, 1)
         query = qkv_k[l, 0]
         keys = qkv_k[l, 1]
         values = qkv_k[l, 2]
@@ -385,11 +570,8 @@
                 for j in range(3):
                     gq_s[l, 4 * h + r, j] = product[128 * r : 128 * r + 128, 128 * j : 128 * j + 128]
         grads_out(l, 0)
-        for h, part in enumerate((left, right)):
-            product = dot_first(mixed_k[l], part).astype(BF)
-            for r in range(4):
-                go_s[l, 4 * h + r] = product[:, 128 * r : 128 * r + 128]
-        grads_out(l, 1)
+        up_relay(l)
+        down_relay(l)
 
         @pl.when(l == 0)
         def _():
@@ -424,13 +606,11 @@
         sum_terms(0, m)
 
     drain(vs_r, v_rs.at[0])
-    place = 2 * col + core
     vh_r[place] = jnp.sum(vs_r[...], axis=0)
 
     @pl.loop(1, 2 * GROUP)
     def _(k):
-        j = lax.rem(place + k, 2 * GROUP)
-        push(vh_r.at[place], vh_r.at[place], v_ss.at[3], v_rs.at[3], (lax.rem(j, 2), row, lax.div(j, 2)))
+        push(vh_r.at[place], vh_r.at[place], v_ss.at[3], v_rs.at[3], row_dev(lax.rem(place + k, 2 * GROUP)))
 
     for m in (0, 1):
         sum_terms(0, m)
@@ -476,8 +656,8 @@
     @pl.loop(0, LAYERS)
     def _(l):
         for m in range(4):
-            fan_sent(own_plane, weights[m][1].at[l], w_ss.at[l, m])
-            fan_sent(own_plane, grads[m][0].at[l], g_ss.at[l, m])
+            weights_sent(l, m)
+            grads_sent(l, m)
             drain(grads[m][2].at[l], x_ss.at[l, m])
         for s in range(4):
             drain(ag.at[l, s, 0, pl.ds(0, 3)], ag_ss.at[l, s])
@@ -490,12 +670,17 @@
 
 
 def finish(*refs):
-    count = len(refs) // 2
-    sems = refs[-1]
-    copies = [pltpu.make_async_copy(refs[n], refs[count + n], sems.at[n]) for n in range(count)]
-    for copy in copies:
+    count = (len(refs) - 2) // 3
+    ins, outs, held = refs[:count], refs[count : 2 * count], refs[2 * count : 3 * count]
+    in_sem, out_sem = refs[3 * count :]
+    loads = [pltpu.make_async_copy(ins[n], held[n], in_sem.at[n]) for n in range(count)]
+    stores = [pltpu.make_async_copy(held[n], outs[n], out_sem.at[n]) for n in range(count)]
+    for copy in loads:
         copy.start()
-    for copy in copies:
+    for load, store in zip(loads, stores):
+        load.wait()
+        store.start()
+    for copy in stores:
         copy.wait()
 
 
@@ -536,7 +721,8 @@
             V((L, 4, 2, 4, 2 * TOK, HALF), BF), V((L, 4, 2, 4, 2 * TOK, HALF), BF),
             V((L, 4, 4, 2 * TOK, HALF), BF), V((L, 4, 4, 2 * TOK, HALF), BF), V((L, 4, 4, 2 * TOK, HALF), BF),
             V((L, 8, 3, 128, 128), BF), V((L, 8, 128, 128), BF), V((L, 8, 128, 512), BF), V((L, 8, 512, 128), BF),
-            V((L, 8, 3, 128, 128), BF), V((L, 8, 128, 128), BF), V((L, 8, 128, 512), BF), V((L, 8, 512, 128), BF),
+            V((L, 8, 3, 128, 128), BF), V((L, 8, 128, 128), BF), V((L, 4, 2, 128, 512), BF), V((L, 2, 4, 512, 128), BF),
+            V((L, 2, 128, 512), BF), V((L, 2, 128, 512), BF), V((L, 4, 512, 128), BF), V((L, 4, 512, 128), BF),
             V((L, 3, 128, 128), F32), V((L, 128, 128), F32), V((L, 128, 512), F32), V((L, 512, 128), F32),
             V((L, 3, 128, 128), F32), V((L, 128, 128), F32), V((L, 128, 512), F32), V((L, 512, 128), F32),
             V((TOK, D), F32), V((L, 2, TOK, D), F32), V((L, 2, TOK, 128), F32), V((L, 2, SEQ, SEQ), F32),
@@ -545,11 +731,11 @@
             V((L, 8, D), F32), V((L, 8, 128), F32),
             V((8, L, 8, 128), F32), V((8, L, 8, 128), F32), V((16, L, 8, 128), F32),
             V((8, L, 8, 128), F32), V((L, 8, 128), F32), V((L, 8, 128), F32),
-            dma((10,)), dma((14,)), dma((2,)), dma((2,)), dma((2,)), dma((2,)), dma((2,)), dma((L, 4)), dma((L, 4)),
+            dma((10,)), dma((14,)), dma((2,)), dma((2,)), dma((2,)), dma((2,)), dma((2,)), dma((L, 4)), dma((L, 4)), dma((L, 4)), dma((L, 4)),
             dma((L, 4)), dma((L, 4, 4)), dma((L, 4)), dma((L, 4)), dma((L, 4, 4)), dma((L, 4)), dma((L, 4, 4)),
-            dma((L, 4)), dma((L, 4)), dma((L, 4)), dma((L, 4)), dma((4,)), dma((4,)),
+            dma((L, 4)), dma((L, 4)), dma((L, 2)), dma((L, 2)), dma((L, 4)), dma((L, 4)), dma((4,)), dma((4,)),
         ],
-        compiler_params=pltpu.CompilerParams(has_side_effects=True, vmem_limit_bytes=60 * 1024 * 1024),
+        compiler_params=pltpu.CompilerParams(collective_id=0, has_side_effects=True, vmem_limit_bytes=60 * 1024 * 1024),
         cost_estimate=pl.CostEstimate(flops=6 * 10**9, bytes_accessed=5 * 10**6, transcendentals=10**6),
     )(*operands)
     results = pl.pallas_call(
@@ -557,7 +743,7 @@
         out_shape=out_shape,
         in_specs=[hbm] * 14,
         out_specs=(hbm,) * 14,
-        scratch_shapes=[dma((14,))],
+        scratch_shapes=[V(a.shape, a.dtype) for a in out_shape] + [dma((14,)), dma((14,))],
     )(*results)
     results = list(results)
     results[2] = results[2].transpose(0, 2, 1, 3)

time: 254 us -> 175 us (0.69)
  Pallas kernels: 254 us -> 174 us
    pallas_call x1, Pallas kernels: 56.7 us -> 2.57 us  [on_device(): pl.pallas_call(finish, out_shape=out_shape, in_specs=[hbm] * 14, out_spec...]
    pallas_call x1, Pallas kernels: 197 us -> 171 us  [on_device(): pl.pallas_call(kernel, out_shape=out_shape, in_specs=[hbm] * 14, out_spec...]
where the time goes in v3:
time: 175 us; the launch traced here: 174 us
  Pallas kernels  174 us (99%)
    pallas_call x1, Pallas kernels, on_device(): pl.pallas_call(kernel, out_shape=out_shape, in_specs=[hbm] * 14, out_spec...  171 us

profile of v3, /device:TPU:1, one launch (start us, length us, event | category | flops | bytes accessed | tf_op | source)
XLA Modules:
  0.0 174.3 jit_solution(5153167522805263459)
XLA Ops:
  0.7 171.1 %shard_map.245 = (bf16[320,128]{1,0:T(8,128)(2,1)}, f32[320,128]{1,0:T(8,128)}, f32[2,3,128,128]{3,2,1,0:T(8,128)}, f32[2,128,128]{2,1,0:T(8,128)}, f32[2,128,51...) custom-call(bf16[320,128]{1,0:T(8,128)(2,1)} %images_h.1, ...), custom_call_target="tpu_custom_call" | custom-call | flops 6000000000 | bytes 5000000 | tf_op jit(solution)/shard_map/pallas_call | solution.py:712
  171.8 2.6 %shard_map.246 = (bf16[320,128]{1,0:T(8,128)(2,1)}, f32[320,128]{1,0:T(8,128)}, f32[2,3,128,128]{3,2,1,0:T(8,128)}, f32[2,128,128]{2,1,0:T(8,128)}, f32[2,128,51...) custom-call(bf16[320,128]{1,0:T(8,128)(2,1)} %get-tuple-element.42.r, ...), custom_call_target="tpu_custom_call" | custom-call | tf_op jit(solution)/shard_map/pallas_call | solution.py:741

commit v4 on v3

--- a/solution.py
+++ b/solution.py
@@ -12,6 +12,9 @@
 LAYERS = 2
 GROUP = 8
 TOK = 40
+ROWS = (40,)
+FIRST = (0,)
+PARTS = (0,)
 SEQ = 320
 D = 1024
 HALF = 512
@@ -47,7 +50,7 @@
     vec_s, vec_g, wq_g, wo_g, wu_g, wd_g,
     ag, rs_s, rs_b, rs_c, rs_r,
     gq_s, go_s, gu_s, gd_s, gq_r, go_r, gu_r, gd_r, gu_c, gu_f, gd_c, gd_f, sq, so, su, sd, tq, to, tu, td,
-    stream, normal_k, scale_k, prob_k, qkv_k, mixed_k, hidden_k, slope_k, grad_k,
+    stream, normal_k, scale_k, prob_k, qkv_k, mixed_k, hidden_k, slope_k, before_k, before_grad_k, grad_k,
     vacc, vcol, vs_s, vs_r, vh_r, vb_r, vt_s, vt_r,
     op_sem, res_sem, in_ss, in_rs, out_ss, out_rs, vec_sem, w_ss, w_rs, wf_ss, wf_rs,
     ag_ss, ag_rs, ag_fs, rs_bs, rs_br, rs_ss, rs_rs, g_ss, g_rs, gf_ss, gf_rs, x_ss, x_rs, v_ss, v_rs,
@@ -192,10 +195,14 @@
     def weight_slot(m, r):
         return r if y_first(m) else 4 * (r % 2) + r // 2
 
+    def qkv_in(l):
+        fan(row, own_plane, lambda j: wqkv.at[l], wq_g.at[l, row], w_ss.at[l, 0], w_rs.at[l, 0], plane_dev)
+
     def weights_in(l):
         @pl.when(own_plane)
         def _():
-            for m, (src, dst) in enumerate(weights):
+            for m in (1, 2, 3):
+                src, dst = weights[m]
                 block = dst.at[l, row if y_first(m) else 4 * yl + z]
                 pltpu.make_async_copy(src.at[l], block, w_rs.at[l, m]).start()
                 for k in (2, 1, 3):
@@ -203,7 +210,7 @@
 
     def weights_relay(l, m):
         dst = weights[m][1]
-        if y_first(m):
+        if m == 3:
             pair = dst.at[l, pl.ds(2 * z, 2)]
             drain(pair, w_rs.at[l, m])
             for k in (2, 1, 3):
@@ -219,7 +226,9 @@
 
     def weight_wait(l, m):
         dst = weights[m][1]
-        if y_first(m):
+        if m == 0:
+            drain(dst.at[l], w_rs.at[l, m])
+        elif m == 3:
             drain(dst.at[l, pl.ds(0, 6)], wf_rs.at[l, m])
         else:
 
@@ -233,12 +242,15 @@
 
     def weights_sent(l, m):
         dst = weights[m][1]
+        if m == 0:
+            fan_sent(own_plane, dst.at[l], w_ss.at[l, m])
+            return
 
         @pl.when(own_plane)
         def _():
             drain(dst.at[l, pl.ds(0, 3)], w_ss.at[l, m])
 
-        if y_first(m):
+        if m == 3:
             drain(dst.at[l, pl.ds(0, 6)], wf_ss.at[l, m])
         else:
 
@@ -247,75 +259,89 @@
                 drain(dst.at[:, pl.ds(0, 6)], wf_ss.at[l, m])
 
     weights_in(0)
-    fetches[9].wait()
-    tiles_fold(1, cot)
-    tiles_in(1)
+    qkv_in(0)
 
     def chip_at(k):
         return lax.rem(x + k, 4)
 
-    def gather_start(l, s, value):
+    def own_rows(p):
+        return slice(FIRST[p], FIRST[p] + ROWS[p])
+
+    def all_rows(p):
+        return slice(GROUP * FIRST[p], GROUP * (FIRST[p] + ROWS[p]))
+
+    def gather_start(l, s, p, value):
         folded = jnp.concatenate([value[:, :HALF], value[:, HALF:]], axis=0).astype(BF)
-        ag[l, s, core, x] = folded
-        mine = ag.at[l, s, core, x]
+        ag[p][l, s, core, x] = folded
+        mine = ag[p].at[l, s, core, x]
         for k in (2, 1, 3):
-            push(mine, mine, ag_ss.at[l, s], ag_rs.at[l, s, k], chip_dev(chip_at(k)))
-        push(mine, mine, ag_fs.at[l, s], ag_rs.at[l, s, 0], sibling)
-
-    def gather_wait(l, s):
+            push(mine, mine, ag_ss.at[l, s, p], ag_rs.at[l, s, p, k], chip_dev(chip_at(k)))
+        push(mine, mine, ag_fs.at[l, s, p], ag_rs.at[l, s, p, 0], sibling)
+
+    def gather_wait(l, s, p):
         for k in (1, 3, 2):
-            came = ag.at[l, s, core, chip_at(4 - k)]
-            drain(came, ag_rs.at[l, s, k])
-            push(came, came, ag_fs.at[l, s], ag_rs.at[l, s, 0], sibling)
-        drain(ag.at[l, s, 0], ag_rs.at[l, s, 0])
-
-    def gather_read(l, s):
-        whole = ag[l, s].astype(F32).reshape(GROUP, 2 * TOK, HALF)
-        left = whole[:, :TOK].reshape(SEQ, HALF).astype(BF)
-        right = whole[:, TOK:].reshape(SEQ, HALF).astype(BF)
+            came = ag[p].at[l, s, core, chip_at(4 - k)]
+            drain(came, ag_rs.at[l, s, p, k])
+            push(came, came, ag_fs.at[l, s, p], ag_rs.at[l, s, p, 0], sibling)
+        drain(ag[p].at[l, s, 0], ag_rs.at[l, s, p, 0])
+
+    def gather_read(l, s, p):
+        rows = ROWS[p]
+        whole = ag[p][l, s].astype(F32).reshape(GROUP, 2 * rows, HALF)
+        left = whole[:, :rows].reshape(GROUP * rows, HALF).astype(BF)
+        right = whole[:, rows:].reshape(GROUP * rows, HALF).astype(BF)
         return left, right
 
-    def scatter_start(l, s, left, right):
-        both = jnp.concatenate([left.reshape(GROUP, TOK, HALF), right.reshape(GROUP, TOK, HALF)], axis=1)
-        rs_s[l, s] = both.astype(BF).reshape(2, 4, 2 * TOK, HALF)
+    def gather_whole(l, s):
+        parts = [gather_read(l, s, p) for p in PARTS]
+        return [jnp.concatenate([part[h] for part in parts], axis=0) for h in range(2)]
+
+    def scatter_start(l, s, p, left, right):
+        rows = ROWS[p]
+        both = jnp.concatenate([left.reshape(GROUP, rows, HALF), right.reshape(GROUP, rows, HALF)], axis=1)
+        rs_s[p][l, s] = both.astype(BF).reshape(2, 4, 2 * rows, HALF)
         for k in (2, 1, 3, 0):
             c = chip_at(k)
-            push(rs_s.at[l, s, 1 - core, c], rs_b.at[l, s, c], rs_bs.at[l, s], rs_br.at[l, s, k], sibling)
-
-    def pair_sum(l, s, k):
+            push(rs_s[p].at[l, s, 1 - core, c], rs_b[p].at[l, s, c], rs_bs.at[l, s, p], rs_br.at[l, s, p, k], sibling)
+
+    def pair_sum(l, s, p, k):
         c = chip_at(k)
-        drain(rs_b.at[l, s, c], rs_br.at[l, s, k])
-        return rs_s[l, s, core, c].astype(F32) + rs_b[l, s, c].astype(F32)
-
-    def scatter_relay(l, s):
+        drain(rs_b[p].at[l, s, c], rs_br.at[l, s, p, k])
+        return rs_s[p][l, s, core, c].astype(F32) + rs_b[p][l, s, c].astype(F32)
+
+    def scatter_relay(l, s, p):
         for k in (2, 1, 3):
-            rs_c[l, s, k] = pair_sum(l, s, k).astype(BF)
-            push(rs_c.at[l, s, k], rs_r.at[l, s, k], rs_ss.at[l, s], rs_rs.at[l, s, k], chip_dev(chip_at(k)))
-
-    def scatter_wait(l, s):
-        total = pair_sum(l, s, 0)
+            rs_c[p][l, s, k] = pair_sum(l, s, p, k).astype(BF)
+            push(rs_c[p].at[l, s, k], rs_r[p].at[l, s, k], rs_ss.at[l, s, p], rs_rs.at[l, s, p, k], chip_dev(chip_at(k)))
+
+    def scatter_wait(l, s, p):
+        rows = ROWS[p]
+        total = pair_sum(l, s, p, 0)
         for k in (1, 3, 2):
-            drain(rs_r.at[l, s, k], rs_rs.at[l, s, k])
-            total += rs_r[l, s, k].astype(F32)
-        return lanes([total[:TOK], total[TOK:]])
+            drain(rs_r[p].at[l, s, k], rs_rs.at[l, s, p, k])
+            total += rs_r[p][l, s, k].astype(F32)
+        return lanes([total[:rows], total[rows:]])
 
     def vec_row(l, i):
         return lanes([vec_g[r, l, i : i + 1, :] for r in range(GROUP)])
 
-    def norm_forward(l, s, value):
+    def norm_forward(l, s, p, value):
         center = jnp.mean(value, axis=1, keepdims=True)
         shifted = value - center
         scaled = lax.rsqrt(jnp.mean(shifted * shifted, axis=1, keepdims=True) + EPS)
         normal = shifted * scaled
-        normal_k[l, s] = normal
-        scale_k[l, s] = jnp.broadcast_to(scaled, (TOK, 128))
+        normal_k[l, s, own_rows(p)] = normal
+        scale_k[l, s, own_rows(p)] = jnp.broadcast_to(scaled, (ROWS[p], 128))
         return normal * vec_row(l, 3 * s) + vec_row(l, 3 * s + 1)
 
-    def norm_backward(l, s, grad_out):
-        normal = normal_k[l, s]
-        scaled = scale_k[l, s][:, 0:1]
-        vacc[l, 3 * s : 3 * s + 1, :] = jnp.sum(grad_out * normal, axis=0, keepdims=True)
-        vacc[l, 3 * s + 1 : 3 * s + 2, :] = jnp.sum(grad_out, axis=0, keepdims=True)
+    def add_row(l, i, value):
+        vacc[l, i : i + 1, :] += jnp.sum(value, axis=0, keepdims=True)
+
+    def norm_backward(l, s, p, grad_out):
+        normal = normal_k[l, s, own_rows(p)]
+        scaled = scale_k[l, s, own_rows(p)][:, 0:1]
+        add_row(l, 3 * s, grad_out * normal)
+        add_row(l, 3 * s + 1, grad_out)
         upstream = grad_out * vec_row(l, 3 * s)
         mean_part = jnp.mean(upstream, axis=1, keepdims=True)
         proj_part = jnp.mean(upstream * normal, axis=1, keepdims=True)
@@ -346,27 +372,43 @@
     drain(in_r.at[0], in_rs.at[0])
     stream[...] = lanes(tiles_read(in_r, 0))
     drain(vec_g, vec_sem.at[1])
+    for p in PARTS:
+        gather_start(0, 0, p, norm_forward(0, 0, p, stream[own_rows(p)]))
+    for m in (1, 2, 3):
+        weights_relay(0, m)
+    fetches[9].wait()
+    tiles_fold(1, cot)
+    tiles_in(1)
+
+    def hidden_part(l, p):
+        left, right = gather_read(l, 1, p)
+        before = dot(left, up_half(l, 0)) + dot(right, up_half(l, 1))
+        shift = vec_g[0, 2 + l]
+        before = before + lanes([shift[2 + j : 3 + j] for j in range(4)])
+        phi = 0.5 * (1.0 + lax.erf(before * ROOT_HALF))
+        hidden = (before * phi).astype(BF)
+        hidden_k[l, all_rows(p)] = hidden
+        before_k[all_rows(p)] = before
+        slope_k[l, all_rows(p)] = phi
+        if p == 0:
+            weight_wait(l, 3)
+        scatter_start(l, 1, p, dot(hidden, down_half(l, 0)), dot(hidden, down_half(l, 1)))
 
     @pl.loop(0, LAYERS)
     def _(l):
-        gather_start(l, 0, norm_forward(l, 0, stream[...]))
-
-        @pl.when(l == 0)
-        def _():
-            for m in (0, 1, 2):
-                weights_relay(0, m)
-
-        gather_wait(l, 0)
-        left, right = gather_read(l, 0)
-        weight_wait(l, 0)
-        projected = dot(left, qkv_half(l, 0)) + dot(right, qkv_half(l, 1))
-        shift = vec_g[0, 2 + l]
-        query = (projected[:, :128] + shift[0:1]).astype(BF)
-        keys = projected[:, 128:256].astype(BF)
-        values = (projected[:, 256:] + shift[1:2]).astype(BF)
-        qkv_k[l, 0] = query
-        qkv_k[l, 1] = keys
-        qkv_k[l, 2] = values
+        for p in PARTS:
+            gather_wait(l, 0, p)
+            left, right = gather_read(l, 0, p)
+            if p == 0:
+                weight_wait(l, 0)
+            projected = dot(left, qkv_half(l, 0)) + dot(right, qkv_half(l, 1))
+            shift = vec_g[0, 2 + l]
+            qkv_k[l, 0, all_rows(p)] = (projected[:, :128] + shift[0:1]).astype(BF)
+            qkv_k[l, 1, all_rows(p)] = projected[:, 128:256].astype(BF)
+            qkv_k[l, 2, all_rows(p)] = (projected[:, 256:] + shift[1:2]).astype(BF)
+        query = qkv_k[l, 0]
+        keys = qkv_k[l, 1]
+        values = qkv_k[l, 2]
         mixed = []
         for h in range(2):
             scores = dot_last(only(h, query), keys) * HEAD_DIM ** -0.5
@@ -377,49 +419,53 @@
         mixed = pick(mixed).astype(BF)
         mixed_k[l] = mixed
         weight_wait(l, 1)
-        scatter_start(l, 0, dot(mixed, out_half(l, 0)), dot(mixed, out_half(l, 1)))
-        scatter_relay(l, 0)
-
+        for p in PARTS:
+            part = mixed[all_rows(p)]
+            scatter_start(l, 0, p, dot(part, out_half(l, 0)), dot(part, out_half(l, 1)))
+        for p in PARTS:
+            scatter_relay(l, 0, p)
         @pl.when(l == 0)
         def _():
-            weights_relay(0, 3)
             weights_in(1)
-
-        base = stream[...] + vec_row(l, 2)
-        middle = base + scatter_wait(l, 0)
-        stream[...] = middle
-        gather_start(l, 1, norm_forward(l, 1, middle))
-        gather_wait(l, 1)
-        left, right = gather_read(l, 1)
-        weight_wait(l, 2)
-        before = dot(left, up_half(l, 0)) + dot(right, up_half(l, 1))
-        shift = vec_g[0, 2 + l]
-        before = before + lanes([shift[2 + j : 3 + j] for j in range(4)])
-        phi = 0.5 * (1.0 + lax.erf(before * ROOT_HALF))
-        hidden = (before * phi).astype(BF)
-        hidden_k[l] = hidden
-        weight_wait(l, 3)
-        scatter_start(l, 1, dot(hidden, down_half(l, 0)), dot(hidden, down_half(l, 1)))
-        scatter_relay(l, 1)
+            qkv_in(1)
+
+        for p in PARTS:
+            middle = stream[own_rows(p)] + vec_row(l, 2) + scatter_wait(l, 0, p)
+            stream[own_rows(p)] = middle
+            gather_start(l, 1, p, norm_forward(l, 1, p, middle))
+        for p in PARTS:
+            gather_wait(l, 1, p)
+            if p == 0:
+                weight_wait(l, 2)
+            else:
+                scatter_relay(l, 1, p - 1)
+            hidden_part(l, p)
+        scatter_relay(l, 1, PARTS[-1])
 
         @pl.when(l == 0)
         def _():
-            for m in range(4):
+            for m in (1, 2, 3):
                 weights_relay(1, m)
-
-        slope_k[l] = phi + before * INV_ROOT_TAU * jnp.exp(-0.5 * before * before)
-        base = stream[...] + vec_row(l, 5)
-        stream[...] = base + scatter_wait(l, 1)
+            drain(in_r.at[1], in_rs.at[1])
+            grad_k[...] = lanes(tiles_read(in_r, 1))
+            for p in PARTS:
+                gather_start(LAYERS - 1, 2, p, grad_k[own_rows(p)])
+
+        before = before_k[...]
+        slope_k[l] = slope_k[l] + before * INV_ROOT_TAU * jnp.exp(-0.5 * before * before)
+
+        @pl.when(l == 0)
+        def _():
+            for p in PARTS:
+                value = stream[own_rows(p)] + vec_row(0, 5) + scatter_wait(0, 1, p)
+                stream[own_rows(p)] = value
+                gather_start(1, 0, p, norm_forward(1, 0, p, value))
 
     def tiles_out(n, value):
         for r in range(GROUP):
             out_f[n, r, 0:TOK] = value[:, 128 * r : 128 * r + 128].astype(BF)
         fan(row, own_tile, lambda j: out_f.at[n, j], out_r.at[n, u], out_ss.at[n], out_rs.at[n], back_dev)
 
-    tiles_out(0, stream[...])
-
-    drain(in_r.at[1], in_rs.at[1])
-    grad_k[...] = lanes(tiles_read(in_r, 1))
     vacc[...] = jnp.zeros_like(vacc)
     vcol[...] = jnp.zeros_like(vcol)
 
@@ -509,41 +555,53 @@
         part[l] = total
         push(part.at[l], other.at[l], x_ss.at[l, m], x_rs.at[l, m], sibling)
 
+    def hidden_back(l, p):
+        left, right = gather_read(l, 2, p)
+        hidden_grad = dot_last(left, down_half(l, 0)) + dot_last(right, down_half(l, 1))
+        before_grad = (hidden_grad * slope_k[l, all_rows(p)]).astype(BF)
+        before_grad_k[all_rows(p)] = before_grad
+        scatter_start(l, 2, p, dot_last(before_grad, up_half(l, 0)), dot_last(before_grad, up_half(l, 1)))
+
     @pl.loop(0, LAYERS)
     def _(step):
         l = LAYERS - 1 - step
-        branch2 = grad_k[...]
-        gather_start(l, 2, branch2)
-        vacc[l, 5:6, :] = jnp.sum(branch2.astype(BF).astype(F32), axis=0, keepdims=True)
-        gather_wait(l, 2)
-        left, right = gather_read(l, 2)
-        hidden_grad = dot_last(left, down_half(l, 0)) + dot_last(right, down_half(l, 1))
-        before_grad = (hidden_grad * slope_k[l]).astype(BF)
-        scatter_start(l, 2, dot_last(before_grad, up_half(l, 0)), dot_last(before_grad, up_half(l, 1)))
-        sums = jnp.sum(before_grad.astype(F32), axis=0, keepdims=True)
-        for j in range(4):
-            vcol[l, 2 + j : 3 + j, :] = sums[:, 128 * j : 128 * j + 128]
-        scatter_relay(l, 2)
-        for h, part in enumerate((left, right)):
+        add_row(l, 5, grad_k[...].astype(BF).astype(F32))
+        for p in PARTS:
+            gather_wait(l, 2, p)
+            if p > 0:
+                scatter_relay(l, 2, p - 1)
+            hidden_back(l, p)
+        scatter_relay(l, 2, PARTS[-1])
+        before_grad = before_grad_k[...]
+        for h, part in enumerate(gather_whole(l, 2)):
             product = dot_first(hidden_k[l], part).astype(BF)
             for r in range(4):
                 gd_s[l, grad_slot(3, 4 * h + r)] = product[:, 128 * r : 128 * r + 128]
         grads_out(l, 3)
-        for h, part in enumerate(gather_read(l, 1)):
+        for h, part in enumerate(gather_whole(l, 1)):
             gu_s[l, 4 * h : 4 * h + 4] = dot_first(part, before_grad).astype(BF).reshape(4, 128, 512)
         grads_out(l, 2)
-        grad_mid = grad_k[...] + norm_backward(l, 1, scatter_wait(l, 2))
-        grad_k[...] = grad_mid
-        gather_start(l, 3, grad_mid)
-        vacc[l, 2:3, :] = jnp.sum(grad_mid.astype(BF).astype(F32), axis=0, keepdims=True)
-        gather_wait(l, 3)
-        left, right = gather_read(l, 3)
-        mixed_grad = (dot_last(left, out_half(l, 0)) + dot_last(right, out_half(l, 1))).astype(BF)
-        for h, part in enumerate((left, right)):
-            product = dot_first(mixed_k[l], part).astype(BF)
-            for r in range(4):
-                go_s[l, 4 * h + r] = product[:, 128 * r : 128 * r + 128]
-        grads_out(l, 1)
+        for p in PARTS:
+            grad_mid = grad_k[own_rows(p)] + norm_backward(l, 1, p, scatter_wait(l, 2, p))
+            grad_k[own_rows(p)] = grad_mid
+            gather_start(l, 3, p, grad_mid)
+        sums = jnp.sum(before_grad.astype(F32), axis=0, keepdims=True)
+        for j in range(4):
+            vcol[l, 2 + j : 3 + j, :] = sums[:, 128 * j : 128 * j + 128]
+        add_row(l, 2, grad_k[...].astype(BF).astype(F32))
+
+        @pl.when(step == 0)
+        def _():
+            for p in PARTS:
+                stream[own_rows(p)] = stream[own_rows(p)] + vec_row(LAYERS - 1, 5) + scatter_wait(LAYERS - 1, 1, p)
+            tiles_out(0, stream[...])
+
+        mixed_grad = []
+        for p in PARTS:
+            gather_wait(l, 3, p)
+            left, right = gather_read(l, 3, p)
+            mixed_grad.append((dot_last(left, out_half(l, 0)) + dot_last(right, out_half(l, 1))).astype(BF))
+        mixed_grad = jnp.concatenate(mixed_grad, axis=0)
         query = qkv_k[l, 0]
         keys = qkv_k[l, 1]
         values = qkv_k[l, 2]
@@ -560,18 +618,26 @@
         keys_grad = (pick(key_grads) * HEAD_DIM ** -0.5).astype(BF)
         values_grad = pick(value_grads).astype(BF)
         joined = lanes([query_grad, keys_grad, values_grad])
-        scatter_start(l, 3, dot_last(joined, qkv_half(l, 0)), dot_last(joined, qkv_half(l, 1)))
-        vcol[l, 0:1, :] = jnp.sum(query_grad.astype(F32), axis=0, keepdims=True)
-        vcol[l, 1:2, :] = jnp.sum(values_grad.astype(F32), axis=0, keepdims=True)
-        scatter_relay(l, 3)
-        for h, part in enumerate(gather_read(l, 0)):
+        for p in PARTS:
+            part = joined[all_rows(p)]
+            scatter_start(l, 3, p, dot_last(part, qkv_half(l, 0)), dot_last(part, qkv_half(l, 1)))
+        for p in PARTS:
+            scatter_relay(l, 3, p)
+        for h, part in enumerate(gather_whole(l, 0)):
             product = dot_first(part, joined).astype(BF)
             for r in range(4):
                 for j in range(3):
                     gq_s[l, 4 * h + r, j] = product[128 * r : 128 * r + 128, 128 * j : 128 * j + 128]
         grads_out(l, 0)
+        for h, part in enumerate(gather_whole(l, 3)):
+            product = dot_first(mixed_k[l], part).astype(BF)
+            for r in range(4):
+                go_s[l, 4 * h + r] = product[:, 128 * r : 128 * r + 128]
+        grads_out(l, 1)
         up_relay(l)
         down_relay(l)
+        vcol[l, 0:1, :] = jnp.sum(query_grad.astype(F32), axis=0, keepdims=True)
+        vcol[l, 1:2, :] = jnp.sum(values_grad.astype(F32), axis=0, keepdims=True)
 
         @pl.when(l == 0)
         def _():
@@ -579,7 +645,12 @@
             for m in (3, 2, 0, 1):
                 sum_terms(1, m)
 
-        grad_k[...] = grad_k[...] + norm_backward(l, 0, scatter_wait(l, 3))
+        for p in PARTS:
+            grad_k[own_rows(p)] = grad_k[own_rows(p)] + norm_backward(l, 0, p, scatter_wait(l, 3, p))
+
+            @pl.when(l > 0)
+            def _():
+                gather_start(l - 1, 2, p, grad_k[own_rows(p)])
 
     tiles_out(1, grad_k[...])
 
@@ -660,10 +731,11 @@
             grads_sent(l, m)
             drain(grads[m][2].at[l], x_ss.at[l, m])
         for s in range(4):
-            drain(ag.at[l, s, 0, pl.ds(0, 3)], ag_ss.at[l, s])
-            drain(ag.at[l, s, 0], ag_fs.at[l, s])
-            drain(rs_b.at[l, s], rs_bs.at[l, s])
-            drain(rs_c.at[l, s, pl.ds(1, 3)], rs_ss.at[l, s])
+            for p in PARTS:
+                drain(ag[p].at[l, s, 0, pl.ds(0, 3)], ag_ss.at[l, s, p])
+                drain(ag[p].at[l, s, 0], ag_fs.at[l, s, p])
+                drain(rs_b[p].at[l, s], rs_bs.at[l, s, p])
+                drain(rs_c[p].at[l, s, pl.ds(1, 3)], rs_ss.at[l, s, p])
 
     for copy in results:
         copy.wait()
@@ -686,6 +758,7 @@
 
 def on_device(images, gain1, bias1, wqkv, qvb, wout, outb, gain2, bias2, wup, upb, wdown, downb, cot):
     L = LAYERS
+    N = len(PARTS)
     wqkv = wqkv.transpose(0, 2, 1, 3)
     hbm = pl.BlockSpec(memory_space=pl.ANY)
     shape = jax.ShapeDtypeStruct
@@ -718,8 +791,8 @@
             V((2, 8, 48, 128), BF), V((2, 8, 48, 128), BF), V((2, 8, 48, 128), BF), V((2, 8, 48, 128), BF),
             V((4, 8, 128), F32), V((8, 4, 8, 128), F32),
             V((L, 8, 3, 128, 128), BF), V((L, 8, 128, 128), BF), V((L, 8, 128, 512), BF), V((L, 8, 512, 128), BF),
-            V((L, 4, 2, 4, 2 * TOK, HALF), BF), V((L, 4, 2, 4, 2 * TOK, HALF), BF),
-            V((L, 4, 4, 2 * TOK, HALF), BF), V((L, 4, 4, 2 * TOK, HALF), BF), V((L, 4, 4, 2 * TOK, HALF), BF),
+            *[tuple(V((L, 4, 2, 4, 2 * rows, HALF), BF) for rows in ROWS) for _ in range(2)],
+            *[tuple(V((L, 4, 4, 2 * rows, HALF), BF) for rows in ROWS) for _ in range(3)],
             V((L, 8, 3, 128, 128), BF), V((L, 8, 128, 128), BF), V((L, 8, 128, 512), BF), V((L, 8, 512, 128), BF),
             V((L, 8, 3, 128, 128), BF), V((L, 8, 128, 128), BF), V((L, 4, 2, 128, 512), BF), V((L, 2, 4, 512, 128), BF),
             V((L, 2, 128, 512), BF), V((L, 2, 128, 512), BF), V((L, 4, 512, 128), BF), V((L, 4, 512, 128), BF),
@@ -727,12 +800,13 @@
             V((L, 3, 128, 128), F32), V((L, 128, 128), F32), V((L, 128, 512), F32), V((L, 512, 128), F32),
             V((TOK, D), F32), V((L, 2, TOK, D), F32), V((L, 2, TOK, 128), F32), V((L, 2, SEQ, SEQ), F32),
             V((L, 3, SEQ, 128), BF), V((L, SEQ, 128), BF), V((L, SEQ, 512), BF), V((L, SEQ, 512), F32),
-            V((TOK, D), F32),
+            V((SEQ, 512), F32), V((SEQ, 512), BF), V((TOK, D), F32),
             V((L, 8, D), F32), V((L, 8, 128), F32),
             V((8, L, 8, 128), F32), V((8, L, 8, 128), F32), V((16, L, 8, 128), F32),
             V((8, L, 8, 128), F32), V((L, 8, 128), F32), V((L, 8, 128), F32),
             dma((10,)), dma((14,)), dma((2,)), dma((2,)), dma((2,)), dma((2,)), dma((2,)), dma((L, 4)), dma((L, 4)), dma((L, 4)), dma((L, 4)),
-            dma((L, 4)), dma((L, 4, 4)), dma((L, 4)), dma((L, 4)), dma((L, 4, 4)), dma((L, 4)), dma((L, 4, 4)),
+            dma((L, 4, N)), dma((L, 4, N, 4)), dma((L, 4, N)), dma((L, 4, N)), dma((L, 4, N, 4)), dma((L, 4, N)),
+            dma((L, 4, N, 4)),
             dma((L, 4)), dma((L, 4)), dma((L, 2)), dma((L, 2)), dma((L, 4)), dma((L, 4)), dma((4,)), dma((4,)),
         ],
         compiler_params=pltpu.CompilerParams(collective_id=0, has_side_effects=True, vmem_limit_bytes=60 * 1024 * 1024),

time: 175 us -> 167 us (0.954)
  Pallas kernels: 174 us -> 166 us
    pallas_call x1, Pallas kernels: 171 us -> 163 us  [on_device(): pl.pallas_call(kernel, out_shape=out_shape, in_specs=[hbm] * 14, out_spec...]
where the time goes in v4:
time: 167 us
  Pallas kernels  166 us (99%)
    pallas_call x1, Pallas kernels, on_device(): pl.pallas_call(kernel, out_shape=out_shape, in_specs=[hbm] * 14, out_spec...  163 us

profile of v4, /device:TPU:1, one launch (start us, length us, event | category | flops | bytes accessed | tf_op | source)
XLA Modules:
  0.0 166.7 jit_solution(16886983226144144044)
XLA Ops:
  0.7 163.4 %shard_map.245 = (bf16[320,128]{1,0:T(8,128)(2,1)}, f32[320,128]{1,0:T(8,128)}, f32[2,3,128,128]{3,2,1,0:T(8,128)}, f32[2,128,128]{2,1,0:T(8,128)}, f32[2,128,51...) custom-call(bf16[320,128]{1,0:T(8,128)(2,1)} %images_h.1, ...), custom_call_target="tpu_custom_call" | custom-call | flops 6000000000 | bytes 5000000 | tf_op jit(solution)/shard_map/pallas_call | solution.py:785
  164.1 2.6 %shard_map.246 = (bf16[320,128]{1,0:T(8,128)(2,1)}, f32[320,128]{1,0:T(8,128)}, f32[2,3,128,128]{3,2,1,0:T(8,128)}, f32[2,128,128]{2,1,0:T(8,128)}, f32[2,128,51...) custom-call(bf16[320,128]{1,0:T(8,128)(2,1)} %get-tuple-element.42.r, ...), custom_call_target="tpu_custom_call" | custom-call | tf_op jit(solution)/shard_map/pallas_call | solution.py:815

commit v5 on v4

--- a/solution.py
+++ b/solution.py
@@ -49,7 +49,7 @@
     in_f, in_r, out_f, out_r,
     vec_s, vec_g, wq_g, wo_g, wu_g, wd_g,
     ag, rs_s, rs_b, rs_c, rs_r,
-    gq_s, go_s, gu_s, gd_s, gq_r, go_r, gu_r, gd_r, gu_c, gu_f, gd_c, gd_f, sq, so, su, sd, tq, to, tu, td,
+    gq_s, go_s, gu_s, gd_s, gq_r, go_r, gu_r, gd_r, gu_c, gu_f, gd_p, gd_q, gd_c, gd_f, sq, so, su, sd, tq, to, tu, td,
     stream, normal_k, scale_k, prob_k, qkv_k, mixed_k, hidden_k, slope_k, before_k, before_grad_k, grad_k,
     vacc, vcol, vs_s, vs_r, vh_r, vb_r, vt_s, vt_r,
     op_sem, res_sem, in_ss, in_rs, out_ss, out_rs, vec_sem, w_ss, w_rs, wf_ss, wf_rs,
@@ -510,12 +510,29 @@
             gu_c[l, j] = total.astype(BF)
         pair_fan(lambda j: gu_c.at[l, j], gu_f.at[l, yl], gf_ss.at[l, 0], gf_rs.at[l, 0])
 
+    keeper = lax.div(z, 2) == core
+
+    def down_pair(l):
+        drain(gd_r.at[l], g_rs.at[l, 3])
+        for j in range(2):
+            theirs = 2 * (1 - core) + j
+            gd_p[l, j] = (gd_r[l, 0, theirs].astype(F32) + gd_r[l, 1, theirs].astype(F32)).astype(BF)
+        push(gd_p.at[l], gd_q.at[l], gf_ss.at[l, 2], gf_rs.at[l, 2], sibling)
+
     def down_relay(l):
-        drain(gd_r.at[l], g_rs.at[l, 3])
-        for j in range(4):
-            gd_c[l, j] = (gd_r[l, 0, j].astype(F32) + gd_r[l, 1, j].astype(F32)).astype(BF)
-        for k in (2, 1, 3):
-            push(gd_c.at[l, z_at(k)], gd_f.at[l, k], gf_ss.at[l, 1], gf_rs.at[l, 1], z_dev(k))
+        drain(gd_q.at[l], gf_rs.at[l, 2])
+        for j in range(2):
+            ours = 2 * core + j
+            total = gd_r[l, 0, ours].astype(F32) + gd_r[l, 1, ours].astype(F32) + gd_q[l, j].astype(F32)
+            gd_c[l, j] = total.astype(BF)
+
+            @pl.when(ours != z)
+            def _():
+                push(gd_c.at[l, j], gd_f.at[l, z], gf_ss.at[l, 1], gf_rs.at[l, 1], (core, 2 * ours + yl, col))
+
+        @pl.when(keeper)
+        def _():
+            gd_f[l, z] = gd_c[l, lax.rem(z, 2)]
 
     def pair_sent(ref, ssem):
         @pl.when(own_plane)
@@ -533,7 +550,15 @@
             pair_sent(gu_c.at[l], gf_ss.at[l, 0])
         elif m == 3:
             pair_sent(dst.at[l], g_ss.at[l, m])
-            drain(gd_f.at[l, pl.ds(1, 3)], gf_ss.at[l, 1])
+            drain(gd_q.at[l], gf_ss.at[l, 2])
+
+            @pl.when(keeper)
+            def _():
+                drain(gd_c.at[l, 0], gf_ss.at[l, 1])
+
+            @pl.when(jnp.logical_not(keeper))
+            def _():
+                drain(gd_c.at[l], gf_ss.at[l, 1])
         else:
             fan_sent(own_plane, src.at[l], g_ss.at[l, m])
 
@@ -543,10 +568,14 @@
             drain(gu_f.at[l], gf_rs.at[l, 0])
             total = gu_f[l, 0].astype(F32) + gu_f[l, 1].astype(F32)
         elif m == 3:
-            drain(gd_f.at[l, pl.ds(1, 3)], gf_rs.at[l, 1])
-            total = gd_c[l, z].astype(F32)
-            for k in (1, 2, 3):
-                total += gd_f[l, k].astype(F32)
+
+            @pl.when(keeper)
+            def _():
+                drain(gd_f.at[l, pl.ds(0, 3)], gf_rs.at[l, 1])
+                part[l] = jnp.sum(gd_f[l].astype(F32), axis=0)
+                push(part.at[l], other.at[l], x_ss.at[l, m], x_rs.at[l, m], sibling)
+
+            return
         else:
             drain(dst.at[l], g_rs.at[l, m])
             total = dst[l, 0].astype(F32)
@@ -605,37 +634,63 @@
         query = qkv_k[l, 0]
         keys = qkv_k[l, 1]
         values = qkv_k[l, 2]
-        value_grads, query_grads, key_grads = [], [], []
+
+        def out_terms():
+            for h, part in enumerate(gather_whole(l, 3)):
+                product = dot_first(mixed_k[l], part).astype(BF)
+                for r in range(4):
+                    go_s[l, 4 * h + r] = product[:, 128 * r : 128 * r + 128]
+            grads_out(l, 1)
+
+        def qkv_term(j, value):
+            for h, part in enumerate(gather_whole(l, 0)):
+                product = dot_first(part, value).astype(BF)
+                for r in range(4):
+                    gq_s[l, 4 * h + r, j] = product[128 * r : 128 * r + 128]
+            fan(
+                row, own_plane, lambda r: gq_s.at[l, r, j], gq_r.at[l, row, j], g_ss.at[l, 0], g_rs.at[l, 0], plane_dev
+            )
+
+        values_grad = pick([dot_first(prob_k[l, h].astype(BF), mixed_grad) for h in range(2)]).astype(BF)
+
+        @pl.when(l == 0)
+        def _():
+            out_terms()
+            qkv_term(2, values_grad)
+
+        query_grads, key_grads = [], []
         for h in range(2):
             probs = prob_k[l, h]
             probs_grad = dot_last(only(h, mixed_grad), values)
             inner = jnp.sum(probs * probs_grad, axis=1, keepdims=True)
             scores_grad = (probs * (probs_grad - inner)).astype(BF)
-            value_grads.append(dot_first(probs.astype(BF), mixed_grad))
             query_grads.append(dot(scores_grad, keys))
             key_grads.append(dot_first(scores_grad, query))
         query_grad = (pick(query_grads) * HEAD_DIM ** -0.5).astype(BF)
         keys_grad = (pick(key_grads) * HEAD_DIM ** -0.5).astype(BF)
-        values_grad = pick(value_grads).astype(BF)
+
+        @pl.when(l == 0)
+        def _():
+            qkv_term(0, query_grad)
+            qkv_term(1, keys_grad)
+
         joined = lanes([query_grad, keys_grad, values_grad])
         for p in PARTS:
             part = joined[all_rows(p)]
             scatter_start(l, 3, p, dot_last(part, qkv_half(l, 0)), dot_last(part, qkv_half(l, 1)))
         for p in PARTS:
             scatter_relay(l, 3, p)
-        for h, part in enumerate(gather_whole(l, 0)):
-            product = dot_first(part, joined).astype(BF)
-            for r in range(4):
-                for j in range(3):
-                    gq_s[l, 4 * h + r, j] = product[128 * r : 128 * r + 128, 128 * j : 128 * j + 128]
-        grads_out(l, 0)
-        for h, part in enumerate(gather_whole(l, 3)):
-            product = dot_first(mixed_k[l], part).astype(BF)
-            for r in range(4):
-                go_s[l, 4 * h + r] = product[:, 128 * r : 128 * r + 128]
-        grads_out(l, 1)
+        down_pair(l)
         up_relay(l)
         down_relay(l)
+
+        @pl.when(l != 0)
+        def _():
+            qkv_term(0, query_grad)
+            qkv_term(1, keys_grad)
+            qkv_term(2, values_grad)
+            out_terms()
+
         vcol[l, 0:1, :] = jnp.sum(query_grad.astype(F32), axis=0, keepdims=True)
         vcol[l, 1:2, :] = jnp.sum(values_grad.astype(F32), axis=0, keepdims=True)
 
@@ -702,8 +757,19 @@
     for m in (3, 2, 0, 1):
         part, other, out, out_hbm = grads[m][2:]
         for l in (1, 0):
-            drain(other.at[l], x_rs.at[l, m])
-            out[l] = part[l] + other[l]
+            if m == 3:
+
+                @pl.when(keeper)
+                def _():
+                    out[l] = part[l]
+
+                @pl.when(jnp.logical_not(keeper))
+                def _():
+                    drain(other.at[l], x_rs.at[l, m])
+                    out[l] = other[l]
+            else:
+                drain(other.at[l], x_rs.at[l, m])
+                out[l] = part[l] + other[l]
         result(out, out_hbm)
 
     drain(vh_r.at[pl.ds(0, 2 * GROUP - 1)], v_rs.at[3])
@@ -729,7 +795,13 @@
         for m in range(4):
             weights_sent(l, m)
             grads_sent(l, m)
-            drain(grads[m][2].at[l], x_ss.at[l, m])
+            if m == 3:
+
+                @pl.when(keeper)
+                def _():
+                    drain(grads[m][2].at[l], x_ss.at[l, m])
+            else:
+                drain(grads[m][2].at[l], x_ss.at[l, m])
         for s in range(4):
             for p in PARTS:
                 drain(ag[p].at[l, s, 0, pl.ds(0, 3)], ag_ss.at[l, s, p])
@@ -795,7 +867,8 @@
             *[tuple(V((L, 4, 4, 2 * rows, HALF), BF) for rows in ROWS) for _ in range(3)],
             V((L, 8, 3, 128, 128), BF), V((L, 8, 128, 128), BF), V((L, 8, 128, 512), BF), V((L, 8, 512, 128), BF),
             V((L, 8, 3, 128, 128), BF), V((L, 8, 128, 128), BF), V((L, 4, 2, 128, 512), BF), V((L, 2, 4, 512, 128), BF),
-            V((L, 2, 128, 512), BF), V((L, 2, 128, 512), BF), V((L, 4, 512, 128), BF), V((L, 4, 512, 128), BF),
+            V((L, 2, 128, 512), BF), V((L, 2, 128, 512), BF), V((L, 2, 512, 128), BF), V((L, 2, 512, 128), BF),
+            V((L, 2, 512, 128), BF), V((L, 4, 512, 128), BF),
             V((L, 3, 128, 128), F32), V((L, 128, 128), F32), V((L, 128, 512), F32), V((L, 512, 128), F32),
             V((L, 3, 128, 128), F32), V((L, 128, 128), F32), V((L, 128, 512), F32), V((L, 512, 128), F32),
             V((TOK, D), F32), V((L, 2, TOK, D), F32), V((L, 2, TOK, 128), F32), V((L, 2, SEQ, SEQ), F32),
@@ -807,7 +880,7 @@
             dma((10,)), dma((14,)), dma((2,)), dma((2,)), dma((2,)), dma((2,)), dma((2,)), dma((L, 4)), dma((L, 4)), dma((L, 4)), dma((L, 4)),
             dma((L, 4, N)), dma((L, 4, N, 4)), dma((L, 4, N)), dma((L, 4, N)), dma((L, 4, N, 4)), dma((L, 4, N)),
             dma((L, 4, N, 4)),
-            dma((L, 4)), dma((L, 4)), dma((L, 2)), dma((L, 2)), dma((L, 4)), dma((L, 4)), dma((4,)), dma((4,)),
+            dma((L, 4)), dma((L, 4)), dma((L, 3)), dma((L, 3)), dma((L, 4)), dma((L, 4)), dma((4,)), dma((4,)),
         ],
         compiler_params=pltpu.CompilerParams(collective_id=0, has_side_effects=True, vmem_limit_bytes=60 * 1024 * 1024),
         cost_estimate=pl.CostEstimate(flops=6 * 10**9, bytes_accessed=5 * 10**6, transcendentals=10**6),

time: 167 us -> 163 us (0.976)
  Pallas kernels: 166 us -> 162 us
    pallas_call x1, Pallas kernels: 163 us -> 160 us  [on_device(): pl.pallas_call(kernel, out_shape=out_shape, in_specs=[hbm] * 14, out_spec...]
where the time goes in v5:
time: 163 us
  Pallas kernels  162 us (99%)
    pallas_call x1, Pallas kernels, on_device(): pl.pallas_call(kernel, out_shape=out_shape, in_specs=[hbm] * 14, out_spec...  160 us

profile of v5, /device:TPU:1, one launch (start us, length us, event | category | flops | bytes accessed | tf_op | source)
XLA Modules:
  0.0 163.1 jit_solution(17435172578004383260)
XLA Ops:
  0.7 159.9 %shard_map.245 = (bf16[320,128]{1,0:T(8,128)(2,1)}, f32[320,128]{1,0:T(8,128)}, f32[2,3,128,128]{3,2,1,0:T(8,128)}, f32[2,128,128]{2,1,0:T(8,128)}, f32[2,128,51...) custom-call(bf16[320,128]{1,0:T(8,128)(2,1)} %images_h.1, ...), custom_call_target="tpu_custom_call" | custom-call | flops 6000000000 | bytes 5000000 | tf_op jit(solution)/shard_map/pallas_call | solution.py:857
  160.5 2.6 %shard_map.246 = (bf16[320,128]{1,0:T(8,128)(2,1)}, f32[320,128]{1,0:T(8,128)}, f32[2,3,128,128]{3,2,1,0:T(8,128)}, f32[2,128,128]{2,1,0:T(8,128)}, f32[2,128,51...) custom-call(bf16[320,128]{1,0:T(8,128)(2,1)} %get-tuple-element.42.r, ...), custom_call_target="tpu_custom_call" | custom-call | tf_op jit(solution)/shard_map/pallas_call | solution.py:888

commit v6 on v5

--- a/solution.py
+++ b/solution.py
@@ -576,6 +576,15 @@
                 push(part.at[l], other.at[l], x_ss.at[l, m], x_rs.at[l, m], sibling)
 
             return
+        elif m == 0:
+            for j in (2, 0, 1):
+                drain(dst.at[l, :, j], g_rs.at[l, 4 + j])
+                total = dst[l, 0, j].astype(F32)
+                for r in range(1, GROUP):
+                    total += dst[l, r, j].astype(F32)
+                part[l, j] = total
+                push(part.at[l, j], other.at[l, j], x_ss.at[l, m], x_rs.at[l, m], sibling)
+            return
         else:
             drain(dst.at[l], g_rs.at[l, m])
             total = dst[l, 0].astype(F32)
@@ -648,7 +657,7 @@
                 for r in range(4):
                     gq_s[l, 4 * h + r, j] = product[128 * r : 128 * r + 128]
             fan(
-                row, own_plane, lambda r: gq_s.at[l, r, j], gq_r.at[l, row, j], g_ss.at[l, 0], g_rs.at[l, 0], plane_dev
+                row, own_plane, lambda r: gq_s.at[l, r, j], gq_r.at[l, row, j], g_ss.at[l, 0], g_rs.at[l, 4 + j], plane_dev
             )
 
         values_grad = pick([dot_first(prob_k[l, h].astype(BF), mixed_grad) for h in range(2)]).astype(BF)
@@ -738,7 +747,7 @@
     def _(k):
         push(vh_r.at[place], vh_r.at[place], v_ss.at[3], v_rs.at[3], row_dev(lax.rem(place + k, 2 * GROUP)))
 
-    for m in (0, 1):
+    for m in (1, 0):
         sum_terms(0, m)
 
     drain(vt_r, v_rs.at[2])
@@ -754,7 +763,7 @@
     gin_o[...] = out_r[1].astype(F32)[:, 0:TOK].reshape(SEQ, 128)
     result(gin_o, gin_h)
 
-    for m in (3, 2, 0, 1):
+    for m in (3, 2, 1, 0):
         part, other, out, out_hbm = grads[m][2:]
         for l in (1, 0):
             if m == 3:
@@ -880,7 +889,7 @@
             dma((10,)), dma((14,)), dma((2,)), dma((2,)), dma((2,)), dma((2,)), dma((2,)), dma((L, 4)), dma((L, 4)), dma((L, 4)), dma((L, 4)),
             dma((L, 4, N)), dma((L, 4, N, 4)), dma((L, 4, N)), dma((L, 4, N)), dma((L, 4, N, 4)), dma((L, 4, N)),
             dma((L, 4, N, 4)),
-            dma((L, 4)), dma((L, 4)), dma((L, 3)), dma((L, 3)), dma((L, 4)), dma((L, 4)), dma((4,)), dma((4,)),
+            dma((L, 4)), dma((L, 7)), dma((L, 3)), dma((L, 3)), dma((L, 4)), dma((L, 4)), dma((4,)), dma((4,)),
         ],
         compiler_params=pltpu.CompilerParams(collective_id=0, has_side_effects=True, vmem_limit_bytes=60 * 1024 * 1024),
         cost_estimate=pl.CostEstimate(flops=6 * 10**9, bytes_accessed=5 * 10**6, transcendentals=10**6),

time: 163 us -> 163 us (level)
  no operation moved by 1% of the time
where the time goes in v6:
time: 163 us
  Pallas kernels  162 us (99%)
    pallas_call x1, Pallas kernels, on_device(): pl.pallas_call(kernel, out_shape=out_shape, in_specs=[hbm] * 14, out_spec...  160 us

profile of v6, /device:TPU:1, one launch (start us, length us, event | category | flops | bytes accessed | tf_op | source)
XLA Modules:
  0.0 163.1 jit_solution(14419900628255554441)
XLA Ops:
  0.7 159.9 %shard_map.245 = (bf16[320,128]{1,0:T(8,128)(2,1)}, f32[320,128]{1,0:T(8,128)}, f32[2,3,128,128]{3,2,1,0:T(8,128)}, f32[2,128,128]{2,1,0:T(8,128)}, f32[2,128,51...) custom-call(bf16[320,128]{1,0:T(8,128)(2,1)} %images_h.1, ...), custom_call_target="tpu_custom_call" | custom-call | flops 6000000000 | bytes 5000000 | tf_op jit(solution)/shard_map/pallas_call | solution.py:866
  160.6 2.6 %shard_map.246 = (bf16[320,128]{1,0:T(8,128)(2,1)}, f32[320,128]{1,0:T(8,128)}, f32[2,3,128,128]{3,2,1,0:T(8,128)}, f32[2,128,128]{2,1,0:T(8,128)}, f32[2,128,51...) custom-call(bf16[320,128]{1,0:T(8,128)(2,1)} %get-tuple-element.42.r, ...), custom_call_target="tpu_custom_call" | custom-call | tf_op jit(solution)/shard_map/pallas_call | solution.py:897
